TPU v7x, 256 devices: a whole 4x4x8 slice. The times are simulated.
256 devices in a mesh: feat: 32 (over z, y), graph: 8 (over x, core).
Axes of the slice: x: 4, y: 4, z: 8, core: 2. Of those that a mesh axis runs over, the one named last changes fastest.
Arguments:
- feats: bfloat16 [768, 131072], P('feat', 'graph'), may hold values from -6 to 6
- front_ids: int32 [8, 8, 4096], P(None, 'graph'), may hold values from 0 to 16383, as said below
- nbr1: int32 [8, 1024, 25], replicated, may hold values from -1 to 32767, as said below
- nbr2: int32 [8, 256, 15], P('graph', 'feat'), may hold values from -1 to 1023, as said below
- w1_self: bfloat16 [768, 512], P('feat'), may hold values from -0.21875 to 0.21875
- w1_neigh: bfloat16 [768, 512], P('feat'), may hold values from -0.21875 to 0.21875
- b1: float32 [512], replicated, may hold values from -3 to 3
- w2_self: bfloat16 [512, 153], replicated, may hold values from -0.25 to 0.25
- w2_neigh: bfloat16 [512, 153], replicated, may hold values from -0.25 to 0.25
- b2: float32 [153], replicated, may hold values from -3 to 3
- dlogits: float32 [8, 256, 153], P('graph', 'feat'), may hold values from -6 to 6
Outputs:
- logits: float32 [8, 256, 153], P('graph', 'feat')
- grad_self: float32 [512, 153], replicated
- grad_neigh: float32 [512, 153], replicated
Inputs may be any that keep to these rules, and one draw needn't show every extreme that they name: `front_ids`: local vertex ids within the named shard. `nbr1`: each target has 1 to 25 valid entries, first in its row, then -1. `nbr2`: each target has 1 to 15 valid entries, first in its row, then -1.
All inputs are finite; a program needn't handle non-finite values.
Results may differ from a plain program's by a relative error of at most 0.0032.
Values may be sent and summed in bfloat16 or wider, within the bound.
A program may use at most 64 MiB of HBM per device.

v0:
```python
import jax
import jax.numpy as jnp
from jax import lax
from jax.sharding import PartitionSpec as P


def count_table(neighbours, base, width):
    positions = base + jnp.arange(width, dtype=jnp.int32)
    total = jnp.zeros((width, neighbours.shape[0]), jnp.float32)
    for slot in range(neighbours.shape[1]):
        total = total + (neighbours[:, slot][None, :] == positions[:, None]).astype(jnp.float32)
    return total.astype(jnp.bfloat16)


def on_device(feats, front_ids, nbr1, nbr2, w1_self, w1_neigh, b1, w2_self, w2_neigh, b2, dlogits):
    owner = lax.axis_index("graph")
    column_group = lax.axis_index("feat")
    groups = lax.axis_size("graph")
    front = front_ids[:, 0, :]
    width_fs = front.shape[1]
    neighbours = lax.dynamic_index_in_dim(nbr1, owner, 0, keepdims=False)
    targets = neighbours.shape[0]
    valid = neighbours >= 0
    degree = jnp.sum(valid, axis=1).astype(jnp.float32)
    local_cols = jnp.take(feats, front, axis=1)
    col_width = local_cols.shape[0]
    contract_first = (((0,), (0,)), ((), ()))
    arrived = lax.all_to_all(local_cols, "graph", split_axis=1, concat_axis=1, tiled=True)

    def add_shard(source, total):
        piece = lax.dynamic_index_in_dim(arrived, source, 1, keepdims=False)
        table = count_table(neighbours, source * width_fs, width_fs)
        return total + jnp.dot(piece, table, preferred_element_type=jnp.float32)

    summed = lax.fori_loop(0, groups, add_shard, jnp.zeros((col_width, targets), jnp.float32))
    own_block = lax.dynamic_index_in_dim(arrived, owner, 1, keepdims=False)
    mean_cols = summed / degree[None, :]
    own_cols = own_block[:, :targets]
    partial_pre = lax.dot_general(
        own_cols, w1_self, contract_first, preferred_element_type=jnp.float32
    )
    partial_pre = partial_pre + lax.dot_general(
        mean_cols, w1_neigh.astype(jnp.float32), contract_first, precision=lax.Precision.HIGHEST
    )
    share = lax.psum_scatter(partial_pre, "feat", scatter_dimension=0, tiled=True)
    share = jnp.maximum(share + b1, 0.0).astype(jnp.bfloat16)
    layer_one = lax.all_gather(share, "feat", axis=0, tiled=True)
    second = nbr2[0]
    seeds = second.shape[0]
    own_seed = lax.dynamic_slice_in_dim(layer_one, column_group * seeds, seeds, 0)
    valid_two = second >= 0
    degree_two = jnp.sum(valid_two, axis=1).astype(jnp.float32)
    picked_two = jnp.take(layer_one, jnp.where(valid_two, second, 0), axis=0)
    mean_two = (
        jnp.sum(jnp.where(valid_two[:, :, None], picked_two.astype(jnp.float32), 0.0), axis=1)
        / degree_two[:, None]
    )
    scores = jnp.dot(own_seed, w2_self, preferred_element_type=jnp.float32)
    scores = (
        scores
        + jnp.dot(mean_two, w2_neigh.astype(jnp.float32), precision=lax.Precision.HIGHEST)
        + b2
    )
    cotangent = dlogits[0]
    grad_s = lax.dot_general(
        own_seed.astype(jnp.float32), cotangent, contract_first, precision=lax.Precision.HIGHEST
    )
    grad_n = lax.dot_general(mean_two, cotangent, contract_first, precision=lax.Precision.HIGHEST)
    grad_s, grad_n = lax.psum((grad_s, grad_n), ("feat", "graph"))
    return (scores[None], grad_s, grad_n)


def solution(mesh):
    in_specs = (
        P("feat", "graph"),
        P(None, "graph", None),
        P(),
        P("graph", "feat", None),
        P("feat", None),
        P("feat", None),
        P(),
        P(),
        P(),
        P(),
        P("graph", "feat", None),
    )
    out_specs = (P("graph", "feat", None), P(), P())
    return jax.shard_map(
        on_device, mesh=mesh, in_specs=in_specs, out_specs=out_specs, check_vma=False
    )
```

profile of v0, /device:TPU:1, one launch (start us, length us, event | category | flops | bytes accessed | tf_op | source)
XLA Modules:
  0.0 1054.8 jit_solution(10119537973705975224)
XLA Ops:
  7.2 1.1 compare_select_fusion
  8.3 1.0 compare_and_fusion
  9.3 4.6 copy.16
  14.0 113.1 %gather_fusion = bf16[32768,24]{1,0:T(8,128)(2,1)} fusion(bf16[24,16384]{0,1:T(8,128)(2,1)} %copy.16, s32[32768]{0:T(1024)S(1)} %broadcast_clamp_fusion), kind=kCustom, calls=%fused_computation | custom fusion | bytes 3276800 | tf_op jit(solution)/shard_map/jit(_take)/gather | solution.py:25
  127.0 6.8 copy.17
  133.8 1.4 select_bitcast_fusion
  135.2 6.7 all-to-all-start
  141.9 0.1 constant_dynamic-slice_fusion
  142.1 0.6 convert_element_type.212
  142.7 20.0 %all-to-all-done = bf16[24,8,4096]{2,0,1:T(8,128)(2,1)S(1)} async-done(((bf16[24,8,4096]{2,0,1:T(8,128)(2,1)}), bf16[24,8,4096]{2,0,1:T(8,128)(2,1)S(1)}, u32[]{:S(2)}, u32[]{:S(2)}) %all-to-all-start) | async-done | bytes 1572896 | tf_op jit(solution)/shard_map/all_to_all | solution.py:28
  162.7 327.0 %while.14 = (s32[]{:T(128)}, f32[24,1024]{1,0:T(8,128)S(1)}, bf16[24,8,4096]{2,0,1:T(8,128)(2,1)S(1)}, s32[1024,25]{0,1:T(8,128)S(1)}, s32[]{:T(128)}, /*index=5*/s32[]{:T(128)}, s32[]{:T(128)}) while((s32[]{:T(128)}, f32[24,1024]{1,0:T(8,128)S(1)}, bf16[24,8,4096]{2,0,1:T(8,128)(2,1)S(1)}, s32[1024,25]{0,1:T(8,128)S(1)}, ...), condition=%wide.region_1.2_spmd.clone, body=%wide.region_0.1_spmd.clone.sunk | while | flops 515952640 | bytes 733299 | solution.py:35
  162.7 0.1 fusion.32
  162.8 40.7 %fusion.34 = f32[24,1024]{1,0:T(8,128)S(1)} fusion(s32[1024]{0:T(1024)S(1)} %bitcast.124, s32[1024]{0:T(1024)S(1)} %bitcast.125, s32[1024]{0:T(1024)S(1)} %bitcast.126, s32[1024]{0:T(1024)S(1)} %bitcast.127, s32[1024]{0:T(1024)S(1)} %bitcast.128, s32[1024]{0:T(1024)S(1)} %bitcast.129, s32[1024]{0:T(1024)S(1)} %bitcast.130, s32[1024]{0:T(1024)S(1)} %bitcast.131, ...), kind=kOutput, calls=%fused_computation.5.clone.1 | convolution fusion | flops 515948544 | bytes 512005 | tf_op jit(solution)/shard_map/while/body/eval_jaxpr/dot_general | solution.py:33
  203.5 0.1 fusion.32
  203.6 40.7 %fusion.34 = f32[24,1024]{1,0:T(8,128)S(1)} fusion(s32[1024]{0:T(1024)S(1)} %bitcast.124, s32[1024]{0:T(1024)S(1)} %bitcast.125, s32[1024]{0:T(1024)S(1)} %bitcast.126, s32[1024]{0:T(1024)S(1)} %bitcast.127, s32[1024]{0:T(1024)S(1)} %bitcast.128, s32[1024]{0:T(1024)S(1)} %bitcast.129, s32[1024]{0:T(1024)S(1)} %bitcast.130, s32[1024]{0:T(1024)S(1)} %bitcast.131, ...), kind=kOutput, calls=%fused_computation.5.clone.1 | convolution fusion | flops 515948544 | bytes 512005 | tf_op jit(solution)/shard_map/while/body/eval_jaxpr/dot_general | solution.py:33
  244.4 0.1 fusion.32
  244.5 40.7 %fusion.34 = f32[24,1024]{1,0:T(8,128)S(1)} fusion(s32[1024]{0:T(1024)S(1)} %bitcast.124, s32[1024]{0:T(1024)S(1)} %bitcast.125, s32[1024]{0:T(1024)S(1)} %bitcast.126, s32[1024]{0:T(1024)S(1)} %bitcast.127, s32[1024]{0:T(1024)S(1)} %bitcast.128, s32[1024]{0:T(1024)S(1)} %bitcast.129, s32[1024]{0:T(1024)S(1)} %bitcast.130, s32[1024]{0:T(1024)S(1)} %bitcast.131, ...), kind=kOutput, calls=%fused_computation.5.clone.1 | convolution fusion | flops 515948544 | bytes 512005 | tf_op jit(solution)/shard_map/while/body/eval_jaxpr/dot_general | solution.py:33
  285.2 0.1 fusion.32
  285.3 40.7 %fusion.34 = f32[24,1024]{1,0:T(8,128)S(1)} fusion(s32[1024]{0:T(1024)S(1)} %bitcast.124, s32[1024]{0:T(1024)S(1)} %bitcast.125, s32[1024]{0:T(1024)S(1)} %bitcast.126, s32[1024]{0:T(1024)S(1)} %bitcast.127, s32[1024]{0:T(1024)S(1)} %bitcast.128, s32[1024]{0:T(1024)S(1)} %bitcast.129, s32[1024]{0:T(1024)S(1)} %bitcast.130, s32[1024]{0:T(1024)S(1)} %bitcast.131, ...), kind=kOutput, calls=%fused_computation.5.clone.1 | convolution fusion | flops 515948544 | bytes 512005 | tf_op jit(solution)/shard_map/while/body/eval_jaxpr/dot_general | solution.py:33
  326.1 0.1 fusion.32
  326.2 40.7 %fusion.34 = f32[24,1024]{1,0:T(8,128)S(1)} fusion(s32[1024]{0:T(1024)S(1)} %bitcast.124, s32[1024]{0:T(1024)S(1)} %bitcast.125, s32[1024]{0:T(1024)S(1)} %bitcast.126, s32[1024]{0:T(1024)S(1)} %bitcast.127, s32[1024]{0:T(1024)S(1)} %bitcast.128, s32[1024]{0:T(1024)S(1)} %bitcast.129, s32[1024]{0:T(1024)S(1)} %bitcast.130, s32[1024]{0:T(1024)S(1)} %bitcast.131, ...), kind=kOutput, calls=%fused_computation.5.clone.1 | convolution fusion | flops 515948544 | bytes 512005 | tf_op jit(solution)/shard_map/while/body/eval_jaxpr/dot_general | solution.py:33
  366.9 0.1 fusion.32
  367.0 40.7 %fusion.34 = f32[24,1024]{1,0:T(8,128)S(1)} fusion(s32[1024]{0:T(1024)S(1)} %bitcast.124, s32[1024]{0:T(1024)S(1)} %bitcast.125, s32[1024]{0:T(1024)S(1)} %bitcast.126, s32[1024]{0:T(1024)S(1)} %bitcast.127, s32[1024]{0:T(1024)S(1)} %bitcast.128, s32[1024]{0:T(1024)S(1)} %bitcast.129, s32[1024]{0:T(1024)S(1)} %bitcast.130, s32[1024]{0:T(1024)S(1)} %bitcast.131, ...), kind=kOutput, calls=%fused_computation.5.clone.1 | convolution fusion | flops 515948544 | bytes 512005 | tf_op jit(solution)/shard_map/while/body/eval_jaxpr/dot_general | solution.py:33
  407.8 0.1 fusion.32
  407.9 40.7 %fusion.34 = f32[24,1024]{1,0:T(8,128)S(1)} fusion(s32[1024]{0:T(1024)S(1)} %bitcast.124, s32[1024]{0:T(1024)S(1)} %bitcast.125, s32[1024]{0:T(1024)S(1)} %bitcast.126, s32[1024]{0:T(1024)S(1)} %bitcast.127, s32[1024]{0:T(1024)S(1)} %bitcast.128, s32[1024]{0:T(1024)S(1)} %bitcast.129, s32[1024]{0:T(1024)S(1)} %bitcast.130, s32[1024]{0:T(1024)S(1)} %bitcast.131, ...), kind=kOutput, calls=%fused_computation.5.clone.1 | convolution fusion | flops 515948544 | bytes 512005 | tf_op jit(solution)/shard_map/while/body/eval_jaxpr/dot_general | solution.py:33
  448.6 0.1 fusion.32
  448.8 40.7 %fusion.34 = f32[24,1024]{1,0:T(8,128)S(1)} fusion(s32[1024]{0:T(1024)S(1)} %bitcast.124, s32[1024]{0:T(1024)S(1)} %bitcast.125, s32[1024]{0:T(1024)S(1)} %bitcast.126, s32[1024]{0:T(1024)S(1)} %bitcast.127, s32[1024]{0:T(1024)S(1)} %bitcast.128, s32[1024]{0:T(1024)S(1)} %bitcast.129, s32[1024]{0:T(1024)S(1)} %bitcast.130, s32[1024]{0:T(1024)S(1)} %bitcast.131, ...), kind=kOutput, calls=%fused_computation.5.clone.1 | convolution fusion | flops 515948544 | bytes 512005 | tf_op jit(solution)/shard_map/while/body/eval_jaxpr/dot_general | solution.py:33
  489.8 0.5 fusion.9
  490.3 2.4 convolution_add_fusion
  492.7 0.0 reduce-scatter.2.cloned.1.call-update
  492.7 0.0 all-gather.2.cloned.1.call-start
  492.8 211.8 %reduce-scatter.2.cloned.1.call-done = f32[32,512]{1,0:T(8,128)} async-done(((f32[1024,512]{1,0:T(8,128)}), f32[32,512]{1,0:T(8,128)}) %reduce-scatter.2.cloned.1.call-update) | async-done | bytes 65552 | tf_op jit(solution)/shard_map/reduce_scatter | solution.py:45
  704.6 1.5 maximum_convert_fusion
  706.1 0.0 all-gather.2.cloned.1.call-update
  706.1 0.0 all-reduce.3.cloned.1.call-start
  706.2 0.1 reshape.124
  706.2 0.1 convert_reduce_fusion.1
  706.4 76.8 %all-gather.2.cloned.1.call-done = bf16[1024,512]{1,0:T(8,128)(2,1)} async-done(((bf16[32,512]{1,0:T(8,128)(2,1)}), bf16[1024,512]{1,0:T(8,128)(2,1)}) %all-gather.2.cloned.1.call-update) | async-done | bytes 1048592 | tf_op jit(solution)/shard_map/all_gather | solution.py:47
  783.2 2.2 gather_fusion.1
  785.4 0.1 reshape.123
  785.5 0.1 select_reduce_fusion
  785.7 1.2 fusion.12
  786.9 1.8 fusion.14
  788.7 0.8 fusion.17
  789.5 0.9 fusion.7
  790.4 254.4 %all-reduce.3.cloned.1.call-done = (f32[512,153]{0,1:T(8,128)}, f32[512,153]{0,1:T(8,128)}) async-done(((f32[512,153]{0,1:T(8,128)}, f32[512,153]{0,1:T(8,128)}), (f32[512,153]{0,1:T(8,128)}, f32[512,153]{0,1:T(8,128)})) %all-reduce.3.cloned.1.call-update) | async-done | bytes 626704 | tf_op jit(solution)/shard_map/psum | solution.py:69
  1044.8 1.7 copy.36
  1046.6 1.7 copy.37
  (47 shorter events, 0.4 us)
Async XLA Ops:
  7.2 134.8 %copy-start = (s32[8,1024,25]{1,0,2:T(8,128)S(1)}, s32[8,1024,25]{1,0,2:T(8,128)}, u32[]{:S(2)}) copy-start(s32[8,1024,25]{1,0,2:T(8,128)} %param.15) | copy-start | bytes 2457604
  135.2 27.5 %all-to-all-start = ((bf16[24,8,4096]{2,0,1:T(8,128)(2,1)}), bf16[24,8,4096]{2,0,1:T(8,128)(2,1)S(1)}, u32[]{:S(2)}, u32[]{:S(2)}) async-start(bf16[24,8,4096]{2,0,1:T(8,128)(2,1)} %select_bitcast_fusion), calls=%async_computation | async-start | bytes 3145728 | tf_op jit(solution)/shard_map/all_to_all | solution.py:28
  141.9 562.6 %reduce-scatter.2.cloned.1.call-start = ((), (), s32[]{:S(2)}) async-start(), calls=%async_computation.2 | async-start | bytes 2162688 | tf_op jit(solution)/shard_map/reduce_scatter | solution.py:45
  162.7 327.1 %copy-start.4 = (bf16[24,512]{1,0:T(8,128)(2,1)S(1)}, bf16[24,512]{1,0:T(8,128)(2,1)}, u32[]{:S(2)}) copy-start(bf16[24,512]{1,0:T(8,128)(2,1)} %param.17) | copy-start | bytes 73732
  162.7 327.6 %copy-start.5 = (bf16[24,512]{1,0:T(8,128)(2,1)S(1)}, bf16[24,512]{1,0:T(8,128)(2,1)}, u32[]{:S(2)}) copy-start(bf16[24,512]{1,0:T(8,128)(2,1)} %param.18) | copy-start | bytes 73732
  162.7 327.6 %copy-start.6 = (f32[1024]{0:T(1024)S(1)}, f32[1024]{0:T(1024)}, u32[]{:S(2)}) copy-start(f32[1024]{0:T(1024)} %convert_element_type.212) | copy-start | bytes 12292
  489.7 214.9 %copy-start.7 = (f32[512]{0:T(512)S(1)}, f32[512]{0:T(512)}, u32[]{:S(2)}) copy-start(f32[512]{0:T(512)} %param.19) | copy-start | bytes 6148
  489.7 216.4 %copy-start.2 = (s32[1,8,15]{2,1,0:T(8,128)S(1)}, s32[1,8,15]{2,1,0:T(8,128)}, u32[]{:S(2)}) copy-start(s32[1,8,15]{2,1,0:T(8,128)} %param.16) | copy-start | bytes 1444
  489.7 295.9 %copy-start.3 = (f32[1,8,153]{2,1,0:T(8,128)S(1)}, f32[1,8,153]{2,1,0:T(8,128)}, u32[]{:S(2)}) copy-start(f32[1,8,153]{2,1,0:T(8,128)} %param.23) | copy-start | bytes 14692
  489.7 298.9 %copy-start.1 = (bf16[512,153]{0,1:T(8,128)(2,1)S(1)}, bf16[512,153]{0,1:T(8,128)(2,1)}, u32[]{:S(2)}) copy-start(bf16[512,153]{0,1:T(8,128)(2,1)} %param.20) | copy-start | bytes 470020
  489.8 299.7 %copy-start.8 = (bf16[512,153]{0,1:T(8,128)(2,1)S(1)}, bf16[512,153]{0,1:T(8,128)(2,1)}, u32[]{:S(2)}) copy-start(bf16[512,153]{0,1:T(8,128)(2,1)} %param.21) | copy-start | bytes 470020
  489.8 299.7 %copy-start.9 = (f32[153]{0:T(256)S(1)}, f32[153]{0:T(256)}, u32[]{:S(2)}) copy-start(f32[153]{0:T(256)} %param.22) | copy-start | bytes 1840
  492.7 290.5 %all-gather.2.cloned.1.call-start = ((), (), s32[]{:S(2)}) async-start(), calls=%async_computation.3 | async-start | bytes 1081344 | tf_op jit(solution)/shard_map/all_gather | solution.py:47
  706.1 338.8 %all-reduce.3.cloned.1.call-start = ((), (), s32[]{:S(2)}) async-start(), calls=%async_computation.4 | async-start | bytes 1310720 | tf_op jit(solution)/shard_map/psum | solution.py:69
Sparse Core Ops, SparseCore 0:
  492.9 211.6 reduce-scatter.1
  708.1 75.1 all-gather.1
  790.3 254.4 all-reduce.2
where the time goes:
time: 1060 us; the launch traced here: 1050 us
  waiting for transfers between devices  563 us (53%)
  matrix products  333 us (31%)
  local copies, waits for them, and re-layouts  131 us (12%)
  between operations  14 us (1%)
    dot_general x8, matrix products, add_shard(): return total + jnp.dot(piece, table, preferred_element_type=jnp.float32)  326 us
    psum x1, waiting for transfers between devices, on_device(): grad_s, grad_n = lax.psum((grad_s, grad_n), ('feat', 'graph'))  254 us
    reduce_scatter x1, waiting for transfers between devices, on_device(): lax.psum_scatter(partial_pre, 'feat', scatter_dimension=0, tiled=True)  212 us
    gather x2, local copies, waits for them, and re-layouts, on_device(): local_cols = jnp.take(feats, front, axis=1)  120 us
    all_gather x1, waiting for transfers between devices, on_device(): layer_one = lax.all_gather(share, 'feat', axis=0, tiled=True)  76.8 us
  transfers between devices with their start and end apart: 4, of which 4 were waited for; matrix products, arithmetic and copies ran while one was open for 0% of the time, Pallas kernels for 0%

commit v1 on v0

v1 whole, which is shorter than its diff:
```python
import functools

import jax
import jax.numpy as jnp
from jax import lax
from jax.experimental import pallas as pl
from jax.experimental.pallas import tpu as pltpu
from jax.sharding import PartitionSpec as P

LANES = 128
FRONT_PAD = 1024
UNROLL = 16
MESH = pl.DeviceIdType.MESH
F32 = jnp.float32
BF16 = jnp.bfloat16
VALID = 1 << 29
RANK_AT = 18


def aligned(index, size):
    return pl.ds(pl.multiple_of(index * size, size), size)


def gather_kernel(
    nb, feats_ref, front_ref, nbr_ref, out_ref, self_ref,
    table, acc, own, one, two, rows_v, front_v, count_v,
    front_s, rows_s, front_i, count_s, sems,
):
    width = feats_ref.shape[0]
    verts = feats_ref.shape[1]
    total = nbr_ref.shape[0]
    per = total // nb
    fan = per // 8
    targets = 8 * LANES
    fs = (front_ref.shape[0] - FRONT_PAD) // nb
    graph = lax.axis_index("graph")

    fetch = pltpu.make_async_copy(front_ref, front_s, sems.at[0])
    fetch.start()

    def turn(i, c):
        block = feats_ref[:, aligned(i, LANES)].astype(F32)
        table[aligned(i, LANES), 0:width] = block.T
        return c

    lax.fori_loop(0, verts // LANES, turn, 0, unroll=4)
    table[verts : verts + 8, :] = jnp.zeros((8, LANES), F32)

    def clear(i, c):
        acc[aligned(i, 64), :] = jnp.zeros((64, LANES), F32)
        return c

    lax.fori_loop(0, nb * targets // 64, clear, 0, unroll=4)
    acc[nb * targets : nb * targets + 8, :] = jnp.zeros((8, LANES), F32)

    below = (
        lax.broadcasted_iota(jnp.int32, (per, per), 0)
        > lax.broadcasted_iota(jnp.int32, (per, per), 1)
    ).astype(F32).astype(BF16)
    sub = lax.broadcasted_iota(jnp.int32, (per, LANES), 0) % 8
    lost = jnp.zeros((1, LANES), jnp.int32)
    for b in range(nb):
        ids = nbr_ref[b * per : (b + 1) * per, :]
        here = (ids // fs == graph) & (ids >= 0)
        gone = jnp.where(here, 0.0, 1.0)
        before = jnp.dot(below, gone.astype(BF16), preferred_element_type=F32)
        rank = before.astype(jnp.int32) + lost
        entry = VALID + rank * (1 << RANK_AT) + (ids % fs + b * fs) * 8 + sub
        one[b * per : (b + 1) * per, :] = jnp.where(here, entry, 0)
        lost = lost + jnp.sum(gone, axis=0, keepdims=True).astype(jnp.int32)
    count = total - lost

    src, dst = one, two
    bits = (total - 1).bit_length()
    block = 64
    for step in range(bits):
        far = 1 << step
        flag = 1 << (RANK_AT + step)
        for at in range(0, total, block):
            stay = src[at : at + block, :]
            have = max(0, min(block, total - at - far))
            kept = jnp.where((stay & flag) != 0, 0, stay)
            if have > 0:
                move = src[at + far : at + far + have, :]
                if have < block:
                    move = jnp.concatenate(
                        [move, jnp.zeros((block - have, LANES), jnp.int32)], axis=0
                    )
                kept = jnp.where((move & flag) != 0, move, kept)
            dst[at : at + block, :] = kept
        src, dst = dst, src

    lane_row = lax.broadcasted_iota(jnp.int32, (LANES, LANES), 1)
    key_row = jnp.broadcast_to(count * LANES, (LANES, LANES)) + lane_row
    key_col = key_row.astype(F32).T
    ahead = jnp.where(key_row.astype(F32) > key_col, 1.0, 0.0)
    place = jnp.sum(ahead, axis=1, keepdims=True).astype(jnp.int32)
    order = jnp.where(place == lane_row, 1.0, 0.0).astype(BF16)

    def shuffle(values):
        got = jnp.dot(values.astype(F32).astype(BF16), order, preferred_element_type=F32)
        return got.astype(jnp.int32)

    wide = jnp.broadcast_to(count, (8, LANES))
    sorted_count = (shuffle(wide // 64) * 64 + shuffle(wide % 64))[0:1]
    lane_id = shuffle(lax.broadcasted_iota(jnp.int32, (8, LANES), 1))[0:1]
    deepest = jnp.max(count)
    fetch.wait()

    def chunk(ch, c):
        entries = src[aligned(ch, LANES), :]
        ident = (entries // 8) % (1 << 15)
        low = shuffle(ident % 256)
        high = shuffle(ident // 256)
        part = shuffle(entries % 8)
        ident = high * 256 + low
        at_row = ch * LANES + lax.broadcasted_iota(jnp.int32, (LANES, LANES), 0)
        live = sorted_count > at_row
        goal = (ident // fs) * targets + part * LANES + lane_id
        rows_v[...] = jnp.where(live, goal, nb * targets)
        front_v[...] = jnp.where(live, ident, nb * fs)
        in_row = jnp.sum(jnp.where(live, 1.0, 0.0), axis=1, keepdims=True).astype(jnp.int32)
        count_v[...] = jnp.broadcast_to((in_row + (UNROLL - 1)) // UNROLL, (LANES, LANES))
        moves = [
            pltpu.make_async_copy(rows_v, rows_s, sems.at[1]),
            pltpu.make_async_copy(front_v, front_i, sems.at[2]),
            pltpu.make_async_copy(count_v, count_s, sems.at[3]),
        ]
        for m in moves:
            m.start()
        for m in moves:
            m.wait()

        def row(r, c):
            def group(g, c):
                base = g * UNROLL
                goals = [rows_s[r, base + u] for u in range(UNROLL)]
                verts_at = [front_s[front_i[r, base + u]] for u in range(UNROLL)]
                got = [table[pl.ds(v, 1), :] for v in verts_at]
                old = [acc[pl.ds(a, 1), :] for a in goals]
                for u in range(UNROLL):
                    acc[pl.ds(goals[u], 1), :] = got[u] + old[u]
                return c

            return lax.fori_loop(0, count_s[r, 0], group, c)

        return lax.fori_loop(0, jnp.minimum(LANES, deepest - ch * LANES), row, c)

    lax.fori_loop(0, (deepest + LANES - 1) // LANES, chunk, 0)

    def mine(i, c):
        base = graph * fs + i * UNROLL
        got = [table[pl.ds(front_s[base + u], 1), :] for u in range(UNROLL)]
        for u in range(UNROLL):
            own[pl.ds(i * UNROLL + u, 1), :] = got[u]
        return c

    lax.fori_loop(0, targets // UNROLL, mine, 0)

    for b in range(nb):
        turned = [
            acc[b * targets + q * LANES : b * targets + (q + 1) * LANES, 0:width].T
            for q in range(8)
        ]
        out_ref[b] = jnp.concatenate(turned, axis=0).astype(BF16)
    turned = [own[q * LANES : (q + 1) * LANES, 0:width].T for q in range(8)]
    self_ref[...] = jnp.concatenate(turned, axis=0).astype(BF16)


def gather(feats, front, nbr, nb):
    width, verts = feats.shape
    total = nbr.shape[0]
    vmem = pl.BlockSpec(memory_space=pltpu.VMEM)
    return pl.pallas_call(
        functools.partial(gather_kernel, nb),
        out_shape=(
            jax.ShapeDtypeStruct((nb, 8 * width, LANES), BF16),
            jax.ShapeDtypeStruct((8 * width, LANES), BF16),
        ),
        in_specs=[vmem, pl.BlockSpec(memory_space=pl.ANY), vmem],
        out_specs=(vmem, vmem),
        scratch_shapes=[
            pltpu.VMEM((verts + 8, LANES), F32),
            pltpu.VMEM((nb * 8 * LANES + 8, LANES), F32),
            pltpu.VMEM((8 * LANES, LANES), F32),
            pltpu.VMEM((total + 64, LANES), jnp.int32),
            pltpu.VMEM((total + 64, LANES), jnp.int32),
            pltpu.VMEM((LANES, LANES), jnp.int32),
            pltpu.VMEM((LANES, LANES), jnp.int32),
            pltpu.VMEM((LANES, LANES), jnp.int32),
            pltpu.SMEM(front.shape, jnp.int32),
            pltpu.SMEM((LANES, LANES), jnp.int32),
            pltpu.SMEM((LANES, LANES), jnp.int32),
            pltpu.SMEM((LANES, LANES), jnp.int32),
            pltpu.SemaphoreType.DMA((4,)),
        ],
        compiler_params=pltpu.CompilerParams(vmem_limit_bytes=40 * 1024 * 1024),
        cost_estimate=pl.CostEstimate(flops=200000000, bytes_accessed=100000000, transcendentals=0),
        name="neighbour_sums",
    )(feats, front, nbr)


def split_dot(ones, wide, dims):
    high = wide.astype(BF16)
    low = (wide - high.astype(F32)).astype(BF16)
    return lax.dot_general(ones, high, dims, preferred_element_type=F32) + lax.dot_general(
        ones, low, dims, preferred_element_type=F32
    )


NN = (((1,), (0,)), ((), ()))
TN = (((0,), (0,)), ((), ()))


def layers_kernel(
    nz, ny,
    part_ref, self_ref, deg_ref, w_ref, b1_ref, w2s_ref, w2n_ref, b2_ref, dl_ref, nbr2_ref,
    logits_ref, grads_ref,
    got1, xs, got2, pre, got3, lp, got4, l2, got5, gp, gotg, gg, gotz, fy,
    s1, r1, s2, r2, s3, r3, s4, r4, s5, r5, sg, rg, sz, rz, sy, ry, sx, rx,
):
    feat = lax.axis_index("feat")
    graph = lax.axis_index("graph")
    ng = part_ref.shape[0]
    z = feat // ny
    y = feat % ny
    width = part_ref.shape[1] // 8
    cdim = w2s_ref.shape[2]

    def at_graph(d):
        return (feat, (graph + d) % ng)

    def at_z(d):
        return (((z + d) % nz) * ny + y, graph)

    def at_y(d):
        return (z * ny + (y + d) % ny, graph)

    barrier = pltpu.get_barrier_semaphore()
    for d in range(1, ng):
        pl.semaphore_signal(barrier, inc=1, device_id=at_graph(d), device_id_type=MESH)
    for d in range(1, nz):
        pl.semaphore_signal(barrier, inc=1, device_id=at_z(d), device_id_type=MESH)
    for d in range(1, ny):
        pl.semaphore_signal(barrier, inc=1, device_id=at_y(d), device_id_type=MESH)
    pl.semaphore_wait(barrier, (ng - 1) + (nz - 1) + (ny - 1))

    def send(src, dst, ssem, rsem, where):
        copy = pltpu.make_async_remote_copy(
            src_ref=src, dst_ref=dst, send_sem=ssem, recv_sem=rsem,
            device_id=where, device_id_type=MESH,
        )
        copy.start()
        return copy

    c1 = [
        send(part_ref.at[(graph + d) % ng], got1.at[d], s1.at[d], r1.at[d], at_graph(d))
        for d in range(1, ng)
    ]

    seeds = dl_ref.shape[0]
    second = nbr2_ref[...]
    deg2 = jnp.sum(jnp.where(second >= 0, 1.0, 0.0), axis=1, keepdims=True)
    spot = z * LANES + lax.broadcasted_iota(jnp.int32, (seeds, LANES), 1)
    hits = jnp.zeros((seeds, LANES), F32)
    for k in range(second.shape[1]):
        hits = hits + jnp.where(second[:, k : k + 1] == spot, 1.0, 0.0)
    hits = hits.astype(BF16)
    row = lax.broadcasted_iota(jnp.int32, (seeds, LANES), 0)
    same = jnp.where(row == spot, 1.0, 0.0).astype(BF16)
    dl = dl_ref[...]

    def exact(ones, wide):
        top = wide.astype(BF16)
        return (
            split_dot(ones, wide - top.astype(F32), TN)
            + lax.dot_general(ones, top, TN, preferred_element_type=F32)
        )

    cot = jnp.concatenate([exact(same, dl), exact(hits, dl / deg2)], axis=1)

    for c in c1:
        c.wait_recv()
    summed = part_ref[graph].astype(F32)
    for d in range(1, ng):
        summed = summed + got1[d].astype(F32)
    for q in range(8):
        xs[q, 0:width, :] = summed[q * width : (q + 1) * width] / deg_ref[q : q + 1, :]
        xs[q, width : 2 * width, :] = self_ref[q * width : (q + 1) * width, :].astype(F32)
    c2 = [
        send(xs.at[(z + d) % nz], got2.at[z], s2.at[d], r2.at[d], at_z(d)) for d in range(1, nz)
    ]
    got2[z] = xs[z]
    for c in c2:
        c.wait_recv()
    x = got2[...].reshape(nz * 2 * width, LANES)
    w = w_ref[...]
    high = x.astype(BF16)
    low = (x - high.astype(F32)).astype(BF16)
    part = lax.dot_general(high, w, TN, preferred_element_type=F32) + lax.dot_general(
        low, w, TN, preferred_element_type=F32
    )
    for k in range(ny):
        pre[k] = part[:, k * LANES : (k + 1) * LANES]
    c3 = [
        send(pre.at[(y + d) % ny], got3.at[d], s3.at[d], r3.at[d], at_y(d)) for d in range(1, ny)
    ]
    for c in c3:
        c.wait_recv()
    h = pre[y]
    for d in range(1, ny):
        h = h + got3[d]
    h = jnp.maximum(h + b1_ref[y], 0.0).astype(BF16)

    g = split_dot(h, cot, TN)
    for k in range(ng):
        gp[k] = g[k * 16 : (k + 1) * 16, :]
    cg = [
        send(gp.at[(graph + d) % ng], gotg.at[d], sg.at[d], rg.at[d], at_graph(d))
        for d in range(1, ng)
    ]

    zs = jnp.dot(h, w2s_ref[y], preferred_element_type=F32)
    zn = jnp.dot(h, w2n_ref[y], preferred_element_type=F32)
    scores = split_dot(hits, zn, NN) / deg2 + split_dot(same, zs, NN)
    for a in range(nz):
        for k in range(ny):
            base = (a * ny + k) * 8
            lp[k, a] = scores[base : base + 8, :]
    c4 = [
        send(lp.at[(y + d) % ny], got4.at[d], s4.at[d], r4.at[d], at_y(d)) for d in range(1, ny)
    ]

    for c in cg:
        c.wait_recv()
    gsum = gp[graph]
    for d in range(1, ng):
        gsum = gsum + gotg[d]
    gg[...] = gsum
    cz = [send(gg, gotz.at[z], sz.at[d], rz.at[d], at_z(d)) for d in range(1, nz)]
    gotz[z] = gsum

    for c in c4:
        c.wait_recv()
    lsum = lp[y]
    for d in range(1, ny):
        lsum = lsum + got4[d]
    l2[...] = lsum
    c5 = [
        send(l2.at[(z + d) % nz], got5.at[d], s5.at[d], r5.at[d], at_z(d)) for d in range(1, nz)
    ]

    for c in cz:
        c.wait_recv()
    whole = gotz[0]
    for k in range(1, nz):
        whole = whole + gotz[k]
    fy[y] = whole.astype(BF16)
    cy = [send(fy.at[y], fy.at[y], sy.at[d], ry.at[d], at_y(d)) for d in range(1, ny)]
    for c in cy:
        c.wait_recv()
    cx = [
        send(fy, grads_ref.at[graph], sx.at[d], rx.at[d], at_graph(d)) for d in range(1, ng)
    ]
    grads_ref[graph] = fy[...]

    for c in c5:
        c.wait_recv()
    final = l2[z] + b2_ref[...]
    for d in range(1, nz):
        final = final + got5[d]
    logits_ref[...] = final

    for c in cx:
        c.wait_recv()
    for c in c1 + c2 + c3 + cg + c4 + cz + c5 + cy + cx:
        c.wait_send()


def layers(nz, ny, part, own, deg, w, b1, w2s, w2n, b2, dl, nbr2):
    ng, rows, _ = part.shape
    width = rows // 8
    cdim = w2s.shape[2]
    vmem = pl.BlockSpec(memory_space=pltpu.VMEM)
    dma = lambda n: pltpu.SemaphoreType.DMA((n,))
    return pl.pallas_call(
        functools.partial(layers_kernel, nz, ny),
        out_shape=(
            jax.ShapeDtypeStruct((8, cdim), F32),
            jax.ShapeDtypeStruct((ng, ny, 16, 2 * cdim), BF16),
        ),
        in_specs=[vmem] * 10,
        out_specs=(vmem, vmem),
        scratch_shapes=[
            pltpu.VMEM((ng, rows, LANES), BF16),
            pltpu.VMEM((8, 2 * width, LANES), F32),
            pltpu.VMEM((nz, 2 * width, LANES), F32),
            pltpu.VMEM((ny, LANES, LANES), F32),
            pltpu.VMEM((ny, LANES, LANES), F32),
            pltpu.VMEM((ny, nz, 8, cdim), F32),
            pltpu.VMEM((ny, nz, 8, cdim), F32),
            pltpu.VMEM((nz, 8, cdim), F32),
            pltpu.VMEM((nz, 8, cdim), F32),
            pltpu.VMEM((ng, 16, 2 * cdim), F32),
            pltpu.VMEM((ng, 16, 2 * cdim), F32),
            pltpu.VMEM((16, 2 * cdim), F32),
            pltpu.VMEM((nz, 16, 2 * cdim), F32),
            pltpu.VMEM((ny, 16, 2 * cdim), BF16),
            dma(ng), dma(ng), dma(nz), dma(nz), dma(ny), dma(ny), dma(ny), dma(ny),
            dma(nz), dma(nz), dma(ng), dma(ng), dma(nz), dma(nz), dma(ny), dma(ny),
            dma(ng), dma(ng),
        ],
        compiler_params=pltpu.CompilerParams(
            collective_id=0, has_side_effects=True, vmem_limit_bytes=40 * 1024 * 1024
        ),
        cost_estimate=pl.CostEstimate(flops=300000000, bytes_accessed=10000000, transcendentals=0),
        name="layers",
    )(part, own, deg, w, b1, w2s, w2n, b2, dl, nbr2)


def on_device(feats, front_ids, nbr1, nbr2, w1_self, w1_neigh, b1, w2_self, w2_neigh, b2, dlogits):
    owner = lax.axis_index("graph")
    nb, targets, fan = nbr1.shape
    width, verts = feats.shape
    hidden, cdim = w2_self.shape
    nz, ny = 8, 4

    groups = [[a * ny + k for a in range(nz)] for k in range(ny)]
    w = lax.all_gather(
        jnp.concatenate([w1_neigh, w1_self], axis=0), "feat",
        axis_index_groups=groups, axis=0, tiled=True,
    )
    side = jnp.concatenate([dlogits[0], nbr2[0].astype(F32)], axis=1)
    side = lax.all_gather(side, "feat", axis=0, tiled=True)
    dl = side[:, :cdim]
    second = side[:, cdim:].astype(jnp.int32)

    front = front_ids[:, 0, :].reshape(-1)
    front = jnp.concatenate([front, jnp.full((FRONT_PAD,), verts, jnp.int32)])
    turned = nbr1.transpose(0, 2, 1)
    own_deg = lax.dynamic_index_in_dim(turned, owner, 0, keepdims=False)
    deg = jnp.sum(own_deg >= 0, axis=0).astype(F32).reshape(8, LANES)
    part, own = gather(feats, front, turned.reshape(nb * fan * 8, LANES), nb)

    b1y = b1.reshape(ny, 1, LANES)
    w2s = w2_self.reshape(ny, LANES, cdim)
    w2n = w2_neigh.reshape(ny, LANES, cdim)
    logits, grads = layers(
        nz, ny, part, own, deg, w, b1y, w2s, w2n, b2.reshape(1, cdim), dl, second
    )
    grads = grads.transpose(1, 0, 2, 3).reshape(hidden, 2 * cdim).astype(F32)
    return (logits[None], grads[:, :cdim], grads[:, cdim:])


def solution(mesh):
    in_specs = (
        P("feat", "graph"),
        P(None, "graph", None),
        P(),
        P("graph", "feat", None),
        P("feat", None),
        P("feat", None),
        P(),
        P(),
        P(),
        P(),
        P("graph", "feat", None),
    )
    out_specs = (P("graph", "feat", None), P(), P())
    return jax.shard_map(
        on_device, mesh=mesh, in_specs=in_specs, out_specs=out_specs, check_vma=False
    )
```

time: 1060 us -> 218 us (0.21)
  waiting for transfers between devices: 563 us -> 0 us
  matrix products: 333 us -> 0 us
  Pallas kernels: 0 us -> 146 us
  local copies, waits for them, and re-layouts: 131 us -> 8.54 us
  blocking collectives: 0 us -> 60.2 us
  between operations: 14 us -> 0.78 us
    dot_general x14 -> x0, matrix products: 333 us -> none  [the longest x8 326 us: add_shard(): return total + jnp.dot(piece, table, preferred_element_type=jnp.float32)]
    psum x1 -> x0, waiting for transfers between devices: 254 us -> none  [on_device(): grad_s, grad_n = lax.psum((grad_s, grad_n), ('feat', 'graph'))]
    reduce_scatter x1 -> x0, waiting for transfers between devices: 212 us -> none  [on_device(): lax.psum_scatter(partial_pre, 'feat', scatter_dimension=0, tiled=True)]
    pallas_call x0 -> x2, Pallas kernels: none -> 146 us  [the longest x1 83.6 us: gather(): pl.pallas_call(functools.partial(gather_kernel, nb), out_shape=(jax.Shape...]
    gather x4 -> x0, local copies, waits for them, and re-layouts: 122 us -> none  [the longest x2 120 us: on_device(): local_cols = jnp.take(feats, front, axis=1)]
    all_gather x1 -> x0, waiting for transfers between devices: 76.8 us -> none  [on_device(): layer_one = lax.all_gather(share, 'feat', axis=0, tiled=True)]
    all_gather x0 -> x2, blocking collectives: none -> 60.2 us  [the longest x1 41.1 us: on_device(): side = lax.all_gather(side, 'feat', axis=0, tiled=True)]
    all_to_all x1 -> x0, waiting for transfers between devices: 20 us -> none  [on_device(): lax.all_to_all(local_cols, 'graph', split_axis=1, concat_axis=1, tiled=True)]
  transfers between devices with their start and end apart: 4 -> 0, of which waited for: 4 -> 0; matrix products, arithmetic and copies ran while one was open for 0% -> 0% of each run, Pallas kernels for 0% -> 0%
where the time goes in v1:
time: 218 us; the launch traced here: 217 us
  Pallas kernels  146 us (67%)
  blocking collectives  60.2 us (28%)
  local copies, waits for them, and re-layouts  8.54 us (4%)
    pallas_call x1, Pallas kernels, gather(): pl.pallas_call(functools.partial(gather_kernel, nb), out_shape=(jax.Shape...  83.6 us
    pallas_call x1, Pallas kernels, layers(): pl.pallas_call(functools.partial(layers_kernel, nz, ny), out_shape=(jax.S...  62.7 us
    all_gather x1, blocking collectives, on_device(): side = lax.all_gather(side, 'feat', axis=0, tiled=True)  41.1 us
    all_gather x1, blocking collectives, on_device(): lax.all_gather(jnp.concatenate([w1_neigh, w1_self], axis=0), 'feat', axis...  19.1 us
    unnamed x25, local copies, waits for them, and re-layouts  6.5 us

profile of v1, /device:TPU:1, one launch (start us, length us, event | category | flops | bytes accessed | tf_op | source)
XLA Modules:
  0.0 217.4 jit_solution(5750704899848295211)
XLA Ops:
  0.6 1.3 fusion
  2.0 1.6 copy.17
  3.6 0.0 copy-start.5
  3.6 0.0 copy-start
  3.6 0.1 reshape.31.nbr_ref
  3.8 0.8 copy-done.5
  4.5 0.3 copy-done
  4.8 0.0 copy-start.9
  4.8 83.6 %neighbour_sums.1 = (bf16[8,192,128]{2,1,0:T(8,128)(2,1)S(1)}, bf16[192,128]{1,0:T(8,128)(2,1)S(1)}) custom-call(bf16[24,16384]{1,0:T(8,128)(2,1)S(1)} %copy-done, s32[33792]{0:T(1024)S(1)} %concatenate.9.front_ref, s32[1600,128]{1,0:T(8,128)S(1)} %reshape.31.nbr_ref), custom_call_target="tpu_custom_call" | custom-call | flops 200000000 | bytes 100000000 | tf_op jit(solution)/shard_map/neighbour_sums/pallas_call | solution.py:174
  88.4 0.0 copy-start.8
  88.4 0.0 copy-done.9
  88.5 0.7 copy-done.8
  89.1 0.1 pad_maximum_fusion.1
  89.2 41.1 %all_gather.7 = f32[256,168]{1,0:T(8,128)S(1)} all-gather(f32[8,168]{1,0:T(8,128)S(1)} %pad_maximum_fusion.1), channel_id=1, replica_groups=mesh['feat'=32,'graph'=8] {'feat'}, dimensions={0}, use_global_device_ids=true | all-gather | bytes 177408 | tf_op jit(solution)/shard_map/all_gather | solution.py:434
  130.3 0.0 copy-start.6
  130.3 0.0 copy-start.7
  130.3 0.1 slice_convert_fusion.nbr2_ref
  130.4 0.6 copy-done.6
  131.1 0.0 copy-done.7
  131.1 0.0 copy-start.3
  131.1 19.1 %all_gather.6.w_ref = bf16[384,512]{1,0:T(8,128)(2,1)S(1)} all-gather(bf16[48,512]{1,0:T(8,128)(2,1)S(1)} %pad_maximum_fusion), channel_id=1, replica_groups={{0,32,64,96,128,160,192,224},{8,40,72,104,136,168,200,232},{16,48,80,11..., dimensions={0}, use_global_device_ids=true | all-gather | bytes 442368 | tf_op jit(solution)/shard_map/all_gather | solution.py:429
  150.2 0.0 copy-done.3
  150.2 0.0 copy-start.4
  150.2 0.1 copy.18
  150.3 0.8 copy-done.4
  151.1 0.1 copy.19
  151.2 0.0 copy-start.1
  151.2 0.0 copy-start.2
  151.2 0.7 copy-done.1
  151.9 0.0 copy-done.2
  151.9 62.7 %layers.1 = (f32[8,153]{1,0:T(8,128)S(1)}, bf16[8,4,16,306]{3,2,1,0:T(8,128)(2,1)S(1)}) custom-call(bf16[8,192,128]{2,1,0:T(8,128)(2,1)S(1)} %get-tuple-element.7.part_ref, bf16[192,128]{1,0:T(8,128)(2,1)S(1)} %get-tuple-element.8.self_ref, f32[8,128]{1,0:T(8,128)S(1)} %convert_bitcast_fusion.2.deg_ref, bf16[384,512]{1,0:T(8,128)(2,1)S(1)} %all_gather.6.w_ref, ...), custom_call_target="tpu_custom_call" | custom-call | flops 300000000 | bytes 10000000 | tf_op jit(solution)/shard_map/layers/pallas_call | solution.py:386
  214.6 0.1 convert_bitcast_fusion
  214.7 0.1 copy.20
  214.8 0.2 fusion.1
  215.0 0.9 copy.21
  215.9 0.9 copy.22
  216.8 0.6 copy.24
  (4 shorter events, 0.0 us)
Async XLA Ops:
  3.6 0.9 copy-start.5
  3.6 1.2 copy-start
  4.8 83.6 %copy-start.9 = (s32[1,8,15]{2,1,0:T(8,128)S(1)}, s32[1,8,15]{2,1,0:T(8,128)}, u32[]{:S(2)}) copy-start(s32[1,8,15]{2,1,0:T(8,128)} %param.14) | copy-start | bytes 1444
  88.4 0.7 copy-start.8
  130.3 0.7 copy-start.6
  130.3 0.8 copy-start.7
  131.1 19.1 %copy-start.3 = (bf16[512,153]{0,1:T(8,128)(2,1)S(1)}, bf16[512,153]{0,1:T(8,128)(2,1)}, u32[]{:S(2)}) copy-start(bf16[512,153]{0,1:T(8,128)(2,1)} %param.18) | copy-start | bytes 470020
  150.2 0.9 copy-start.4
  151.2 0.7 copy-start.1
  151.2 0.7 copy-start.2

commit v2 on v1

--- a/solution.py
+++ b/solution.py
@@ -8,8 +8,11 @@
 from jax.sharding import PartitionSpec as P
 
 LANES = 128
+UNROLL = 8
+CHUNK = 32
 FRONT_PAD = 1024
-UNROLL = 16
+WORD_BITS = 16
+WORD = 1 << WORD_BITS
 MESH = pl.DeviceIdType.MESH
 F32 = jnp.float32
 BF16 = jnp.bfloat16
@@ -22,20 +25,19 @@
 
 
 def gather_kernel(
-    nb, feats_ref, front_ref, nbr_ref, out_ref, self_ref,
-    table, acc, own, one, two, rows_v, front_v, count_v,
-    front_s, rows_s, front_i, count_s, sems,
+    nb, feats_ref, front_ref, nbr_ref, out_ref, self_ref, deg_ref,
+    table, acc, own, one, two, lists_v, lists_s, front_s, sems, front_sem,
 ):
     width = feats_ref.shape[0]
     verts = feats_ref.shape[1]
     total = nbr_ref.shape[0]
     per = total // nb
-    fan = per // 8
     targets = 8 * LANES
     fs = (front_ref.shape[0] - FRONT_PAD) // nb
+    fs_bits = fs.bit_length() - 1
     graph = lax.axis_index("graph")
 
-    fetch = pltpu.make_async_copy(front_ref, front_s, sems.at[0])
+    fetch = pltpu.make_async_copy(front_ref, front_s, front_sem)
     fetch.start()
 
     def turn(i, c):
@@ -52,6 +54,12 @@
 
     lax.fori_loop(0, nb * targets // 64, clear, 0, unroll=4)
     acc[nb * targets : nb * targets + 8, :] = jnp.zeros((8, LANES), F32)
+
+    degree = jnp.zeros((8, LANES), F32)
+    for k in range(per // 8):
+        ids = nbr_ref[pl.ds(pl.multiple_of(graph * per + k * 8, 8), 8), :]
+        degree = degree + jnp.where(ids >= 0, 1.0, 0.0)
+    deg_ref[...] = degree
 
     below = (
         lax.broadcasted_iota(jnp.int32, (per, per), 0)
@@ -61,11 +69,11 @@
     lost = jnp.zeros((1, LANES), jnp.int32)
     for b in range(nb):
         ids = nbr_ref[b * per : (b + 1) * per, :]
-        here = (ids // fs == graph) & (ids >= 0)
+        here = (ids >> fs_bits) == graph
         gone = jnp.where(here, 0.0, 1.0)
         before = jnp.dot(below, gone.astype(BF16), preferred_element_type=F32)
         rank = before.astype(jnp.int32) + lost
-        entry = VALID + rank * (1 << RANK_AT) + (ids % fs + b * fs) * 8 + sub
+        entry = VALID + rank * (1 << RANK_AT) + ((ids & (fs - 1)) + b * fs) * 8 + sub
         one[b * per : (b + 1) * per, :] = jnp.where(here, entry, 0)
         lost = lost + jnp.sum(gone, axis=0, keepdims=True).astype(jnp.int32)
     count = total - lost
@@ -104,49 +112,77 @@
     wide = jnp.broadcast_to(count, (8, LANES))
     sorted_count = (shuffle(wide // 64) * 64 + shuffle(wide % 64))[0:1]
     lane_id = shuffle(lax.broadcasted_iota(jnp.int32, (8, LANES), 1))[0:1]
+    count_col = jnp.broadcast_to(sorted_count.astype(F32), (LANES, LANES)).T
     deepest = jnp.max(count)
+    chunks = (deepest + CHUNK - 1) // CHUNK
+
+    def prepare(ch, slot):
+        entries = src[aligned(ch, CHUNK), :]
+        ident = (entries >> 3) & (nb * fs - 1)
+        ident = shuffle(ident >> 8) * 256 + shuffle(ident & 255)
+        group = shuffle(entries & 7)
+        at_row = ch * CHUNK + lax.broadcasted_iota(jnp.int32, (CHUNK, LANES), 0)
+        live = sorted_count > at_row
+        goal = (ident >> fs_bits) * targets + group * LANES + lane_id
+        word = jnp.where(live, goal * WORD + ident, nb * targets * WORD + nb * fs)
+        lists_v[slot, 0:CHUNK, :] = word
+        row_at = (ch * CHUNK + lane_row).astype(F32)
+        in_row = jnp.sum(jnp.where(count_col > row_at, 1.0, 0.0), axis=0, keepdims=True)
+        groups = (in_row.astype(jnp.int32) + (UNROLL - 1)) // UNROLL
+        lists_v[slot, CHUNK : CHUNK + 8, :] = jnp.broadcast_to(groups, (8, LANES))
+
+    def transfer(slot):
+        return pltpu.make_async_copy(
+            lists_v.at[slot],
+            lists_s.at[pl.ds(pl.multiple_of(slot * (CHUNK + 8), 8), CHUNK + 8)],
+            sems.at[slot],
+        )
+
+    @pl.when(chunks > 0)
+    def _():
+        prepare(0, 0)
+        transfer(0).start()
+
     fetch.wait()
 
     def chunk(ch, c):
-        entries = src[aligned(ch, LANES), :]
-        ident = (entries // 8) % (1 << 15)
-        low = shuffle(ident % 256)
-        high = shuffle(ident // 256)
-        part = shuffle(entries % 8)
-        ident = high * 256 + low
-        at_row = ch * LANES + lax.broadcasted_iota(jnp.int32, (LANES, LANES), 0)
-        live = sorted_count > at_row
-        goal = (ident // fs) * targets + part * LANES + lane_id
-        rows_v[...] = jnp.where(live, goal, nb * targets)
-        front_v[...] = jnp.where(live, ident, nb * fs)
-        in_row = jnp.sum(jnp.where(live, 1.0, 0.0), axis=1, keepdims=True).astype(jnp.int32)
-        count_v[...] = jnp.broadcast_to((in_row + (UNROLL - 1)) // UNROLL, (LANES, LANES))
-        moves = [
-            pltpu.make_async_copy(rows_v, rows_s, sems.at[1]),
-            pltpu.make_async_copy(front_v, front_i, sems.at[2]),
-            pltpu.make_async_copy(count_v, count_s, sems.at[3]),
-        ]
-        for m in moves:
-            m.start()
-        for m in moves:
-            m.wait()
+        slot = ch & 1
+        base = slot * (CHUNK + 8)
+        transfer(slot).wait()
+
+        @pl.when(ch + 1 < chunks)
+        def _():
+            prepare(ch + 1, 1 - slot)
+            transfer(1 - slot).start()
 
         def row(r, c):
-            def group(g, c):
-                base = g * UNROLL
-                goals = [rows_s[r, base + u] for u in range(UNROLL)]
-                verts_at = [front_s[front_i[r, base + u]] for u in range(UNROLL)]
-                got = [table[pl.ds(v, 1), :] for v in verts_at]
+            def group(g):
+                words = [lists_s[at, g * UNROLL + u] for u in range(UNROLL)]
+                got = [table[pl.ds(front_s[w & (WORD - 1)], 1), :] for w in words]
+                goals = [w >> WORD_BITS for w in words]
                 old = [acc[pl.ds(a, 1), :] for a in goals]
                 for u in range(UNROLL):
                     acc[pl.ds(goals[u], 1), :] = got[u] + old[u]
-                return c
-
-            return lax.fori_loop(0, count_s[r, 0], group, c)
-
-        return lax.fori_loop(0, jnp.minimum(LANES, deepest - ch * LANES), row, c)
-
-    lax.fori_loop(0, (deepest + LANES - 1) // LANES, chunk, 0)
+
+            groups = lists_s[base + CHUNK, r]
+            at = base + r
+            every = LANES // UNROLL
+
+            @pl.when(groups == every)
+            def _():
+                for g in range(every):
+                    group(g)
+
+            @pl.when(groups < every)
+            def _():
+                for g in range(every):
+                    pl.when(g < groups)(functools.partial(group, g))
+
+            return c
+
+        return lax.fori_loop(0, jnp.minimum(CHUNK, deepest - ch * CHUNK), row, c)
+
+    lax.fori_loop(0, chunks, chunk, 0)
 
     def mine(i, c):
         base = graph * fs + i * UNROLL
@@ -176,23 +212,21 @@
         out_shape=(
             jax.ShapeDtypeStruct((nb, 8 * width, LANES), BF16),
             jax.ShapeDtypeStruct((8 * width, LANES), BF16),
+            jax.ShapeDtypeStruct((8, LANES), F32),
         ),
         in_specs=[vmem, pl.BlockSpec(memory_space=pl.ANY), vmem],
-        out_specs=(vmem, vmem),
+        out_specs=(vmem, vmem, vmem),
         scratch_shapes=[
             pltpu.VMEM((verts + 8, LANES), F32),
             pltpu.VMEM((nb * 8 * LANES + 8, LANES), F32),
             pltpu.VMEM((8 * LANES, LANES), F32),
             pltpu.VMEM((total + 64, LANES), jnp.int32),
             pltpu.VMEM((total + 64, LANES), jnp.int32),
-            pltpu.VMEM((LANES, LANES), jnp.int32),
-            pltpu.VMEM((LANES, LANES), jnp.int32),
-            pltpu.VMEM((LANES, LANES), jnp.int32),
+            pltpu.VMEM((2, CHUNK + 8, LANES), jnp.int32),
+            pltpu.SMEM((2 * (CHUNK + 8), LANES), jnp.int32),
             pltpu.SMEM(front.shape, jnp.int32),
-            pltpu.SMEM((LANES, LANES), jnp.int32),
-            pltpu.SMEM((LANES, LANES), jnp.int32),
-            pltpu.SMEM((LANES, LANES), jnp.int32),
-            pltpu.SemaphoreType.DMA((4,)),
+            pltpu.SemaphoreType.DMA((2,)),
+            pltpu.SemaphoreType.DMA,
         ],
         compiler_params=pltpu.CompilerParams(vmem_limit_bytes=40 * 1024 * 1024),
         cost_estimate=pl.CostEstimate(flops=200000000, bytes_accessed=100000000, transcendentals=0),
@@ -214,10 +248,10 @@
 
 def layers_kernel(
     nz, ny,
-    part_ref, self_ref, deg_ref, w_ref, b1_ref, w2s_ref, w2n_ref, b2_ref, dl_ref, nbr2_ref,
+    part_ref, self_ref, deg_ref, w_ref, b1_ref, w2s_ref, w2n_ref, b2_ref, side_ref,
     logits_ref, grads_ref,
-    got1, xs, got2, pre, got3, lp, got4, l2, got5, gp, gotg, gg, gotz, fy,
-    s1, r1, s2, r2, s3, r3, s4, r4, s5, r5, sg, rg, sz, rz, sy, ry, sx, rx,
+    gotw, sv, sall, got1, xs, got2, pre, got3, lp, got4, l2, got5, gp, gotg, gg, gotz, fy,
+    sw, rw, sf, rf, sa, ra, sb, rb, s1, r1, s2, r2, s3, r3, s4, r4, s5, r5, sg, rg, sz, rz, sy, ry, sx, rx,
 ):
     feat = lax.axis_index("feat")
     graph = lax.axis_index("graph")
@@ -258,17 +292,59 @@
         for d in range(1, ng)
     ]
 
-    seeds = dl_ref.shape[0]
-    second = nbr2_ref[...]
+    ca = [send(side_ref, sv.at[z], sa.at[d], ra.at[d], at_z(d)) for d in range(1, nz)]
+    sv[z] = side_ref[...]
+
+    core = graph % 2
+    sibling = (feat, graph + 1 - 2 * core)
+
+    def weight_copy(d):
+        return pltpu.make_async_remote_copy(
+            src_ref=w_ref, dst_ref=gotw.at[z], send_sem=sw.at[d], recv_sem=rw.at[d],
+            device_id=at_z(d), device_id_type=MESH,
+        )
+
+    def weight_pass(d):
+        block = gotw.at[(z - d + nz) % nz]
+        return pltpu.make_async_remote_copy(
+            src_ref=block, dst_ref=block, send_sem=sf.at[d], recv_sem=rf.at[d],
+            device_id=sibling, device_id_type=MESH,
+        )
+
+    @pl.when(z % 2 == core)
+    def _():
+        for d in range(1, nz):
+            weight_copy(d).start()
+
+    gotw[z] = w_ref[...]
+
+    for c in ca:
+        c.wait_recv()
+    cb = [send(sv, sall.at[y], sb.at[d], rb.at[d], at_y(d)) for d in range(1, ny)]
+    sall[y] = sv[...]
+
+    for d in range(1, nz):
+        @pl.when((z + d) % 2 == core)
+        def _():
+            weight_copy(d).wait_recv()
+            weight_pass(d).start()
+
+    for c in cb:
+        c.wait_recv()
+
+    side = sall[...].reshape(ny * nz * 8, side_ref.shape[1])
+    seeds = ny * nz * 8
+    dl = side[:, :cdim]
+    second = side[:, cdim:].astype(jnp.int32)
     deg2 = jnp.sum(jnp.where(second >= 0, 1.0, 0.0), axis=1, keepdims=True)
     spot = z * LANES + lax.broadcasted_iota(jnp.int32, (seeds, LANES), 1)
     hits = jnp.zeros((seeds, LANES), F32)
     for k in range(second.shape[1]):
         hits = hits + jnp.where(second[:, k : k + 1] == spot, 1.0, 0.0)
     hits = hits.astype(BF16)
-    row = lax.broadcasted_iota(jnp.int32, (seeds, LANES), 0)
+    at = lax.broadcasted_iota(jnp.int32, (seeds, LANES), 0)
+    row = ((at // 8) % nz) * (ny * 8) + (at // (8 * nz)) * 8 + at % 8
     same = jnp.where(row == spot, 1.0, 0.0).astype(BF16)
-    dl = dl_ref[...]
 
     def exact(ones, wide):
         top = wide.astype(BF16)
@@ -294,7 +370,11 @@
     for c in c2:
         c.wait_recv()
     x = got2[...].reshape(nz * 2 * width, LANES)
-    w = w_ref[...]
+    for d in range(1, nz):
+        @pl.when((z + d) % 2 != core)
+        def _():
+            weight_pass(d).wait_recv()
+    w = gotw[...].reshape(nz * 2 * width, w_ref.shape[1])
     high = x.astype(BF16)
     low = (x - high.astype(F32)).astype(BF16)
     part = lax.dot_general(high, w, TN, preferred_element_type=F32) + lax.dot_general(
@@ -323,10 +403,7 @@
     zs = jnp.dot(h, w2s_ref[y], preferred_element_type=F32)
     zn = jnp.dot(h, w2n_ref[y], preferred_element_type=F32)
     scores = split_dot(hits, zn, NN) / deg2 + split_dot(same, zs, NN)
-    for a in range(nz):
-        for k in range(ny):
-            base = (a * ny + k) * 8
-            lp[k, a] = scores[base : base + 8, :]
+    lp[...] = scores.reshape(ny, nz, 8, cdim)
     c4 = [
         send(lp.at[(y + d) % ny], got4.at[d], s4.at[d], r4.at[d], at_y(d)) for d in range(1, ny)
     ]
@@ -373,11 +450,21 @@
 
     for c in cx:
         c.wait_recv()
-    for c in c1 + c2 + c3 + cg + c4 + cz + c5 + cy + cx:
+    for c in ca + cb + c1 + c2 + c3 + cg + c4 + cz + c5 + cy + cx:
         c.wait_send()
 
-
-def layers(nz, ny, part, own, deg, w, b1, w2s, w2n, b2, dl, nbr2):
+    @pl.when(z % 2 == core)
+    def _():
+        for d in range(1, nz):
+            weight_copy(d).wait_send()
+
+    for d in range(1, nz):
+        @pl.when((z + d) % 2 == core)
+        def _():
+            weight_pass(d).wait_send()
+
+
+def layers(nz, ny, part, own, deg, w, b1, w2s, w2n, b2, side):
     ng, rows, _ = part.shape
     width = rows // 8
     cdim = w2s.shape[2]
@@ -389,9 +476,12 @@
             jax.ShapeDtypeStruct((8, cdim), F32),
             jax.ShapeDtypeStruct((ng, ny, 16, 2 * cdim), BF16),
         ),
-        in_specs=[vmem] * 10,
+        in_specs=[vmem] * 9,
         out_specs=(vmem, vmem),
         scratch_shapes=[
+            pltpu.VMEM((nz, 2 * width, w.shape[1]), BF16),
+            pltpu.VMEM((nz,) + side.shape, F32),
+            pltpu.VMEM((ny, nz) + side.shape, F32),
             pltpu.VMEM((ng, rows, LANES), BF16),
             pltpu.VMEM((8, 2 * width, LANES), F32),
             pltpu.VMEM((nz, 2 * width, LANES), F32),
@@ -406,6 +496,7 @@
             pltpu.VMEM((16, 2 * cdim), F32),
             pltpu.VMEM((nz, 16, 2 * cdim), F32),
             pltpu.VMEM((ny, 16, 2 * cdim), BF16),
+            dma(nz), dma(nz), dma(nz), dma(nz), dma(nz), dma(nz), dma(ny), dma(ny),
             dma(ng), dma(ng), dma(nz), dma(nz), dma(ny), dma(ny), dma(ny), dma(ny),
             dma(nz), dma(nz), dma(ng), dma(ng), dma(nz), dma(nz), dma(ny), dma(ny),
             dma(ng), dma(ng),
@@ -415,38 +506,28 @@
         ),
         cost_estimate=pl.CostEstimate(flops=300000000, bytes_accessed=10000000, transcendentals=0),
         name="layers",
-    )(part, own, deg, w, b1, w2s, w2n, b2, dl, nbr2)
+    )(part, own, deg, w, b1, w2s, w2n, b2, side)
 
 
 def on_device(feats, front_ids, nbr1, nbr2, w1_self, w1_neigh, b1, w2_self, w2_neigh, b2, dlogits):
-    owner = lax.axis_index("graph")
     nb, targets, fan = nbr1.shape
     width, verts = feats.shape
     hidden, cdim = w2_self.shape
     nz, ny = 8, 4
 
-    groups = [[a * ny + k for a in range(nz)] for k in range(ny)]
-    w = lax.all_gather(
-        jnp.concatenate([w1_neigh, w1_self], axis=0), "feat",
-        axis_index_groups=groups, axis=0, tiled=True,
-    )
+    w = jnp.concatenate([w1_neigh, w1_self], axis=0)
     side = jnp.concatenate([dlogits[0], nbr2[0].astype(F32)], axis=1)
-    side = lax.all_gather(side, "feat", axis=0, tiled=True)
-    dl = side[:, :cdim]
-    second = side[:, cdim:].astype(jnp.int32)
-
-    front = front_ids[:, 0, :].reshape(-1)
+
+    front = front_ids.reshape(-1)
     front = jnp.concatenate([front, jnp.full((FRONT_PAD,), verts, jnp.int32)])
     turned = nbr1.transpose(0, 2, 1)
-    own_deg = lax.dynamic_index_in_dim(turned, owner, 0, keepdims=False)
-    deg = jnp.sum(own_deg >= 0, axis=0).astype(F32).reshape(8, LANES)
-    part, own = gather(feats, front, turned.reshape(nb * fan * 8, LANES), nb)
+    part, own, deg = gather(feats, front, turned.reshape(nb * fan * 8, LANES), nb)
 
     b1y = b1.reshape(ny, 1, LANES)
     w2s = w2_self.reshape(ny, LANES, cdim)
     w2n = w2_neigh.reshape(ny, LANES, cdim)
     logits, grads = layers(
-        nz, ny, part, own, deg, w, b1y, w2s, w2n, b2.reshape(1, cdim), dl, second
+        nz, ny, part, own, deg, w, b1y, w2s, w2n, b2.reshape(1, cdim), side
     )
     grads = grads.transpose(1, 0, 2, 3).reshape(hidden, 2 * cdim).astype(F32)
     return (logits[None], grads[:, :cdim], grads[:, cdim:])

time: 218 us -> 120 us (0.55)
  blocking collectives: 60.2 us -> 0 us
  Pallas kernels: 146 us -> 110 us
    all_gather x2 -> x0, blocking collectives: 60.2 us -> none  [the longest x1 41.1 us: on_device(): side = lax.all_gather(side, 'feat', axis=0, tiled=True)]
    pallas_call x1, Pallas kernels: 83.6 us -> 49.8 us  [gather(): pl.pallas_call(functools.partial(gather_kernel, nb), out_shape=(jax.Shape...]
    pallas_call x1, Pallas kernels: 62.7 us -> 60.1 us  [layers(): pl.pallas_call(functools.partial(layers_kernel, nz, ny), out_shape=(jax.S...]
where the time goes in v2:
time: 120 us
  Pallas kernels  110 us (92%)
  local copies, waits for them, and re-layouts  9.2 us (8%)
    pallas_call x1, Pallas kernels, layers(): pl.pallas_call(functools.partial(layers_kernel, nz, ny), out_shape=(jax.S...  60.1 us
    pallas_call x1, Pallas kernels, gather(): pl.pallas_call(functools.partial(gather_kernel, nb), out_shape=(jax.Shape...  49.8 us
    unnamed x25, local copies, waits for them, and re-layouts  7.18 us

profile of v2, /device:TPU:1, one launch (start us, length us, event | category | flops | bytes accessed | tf_op | source)
XLA Modules:
  0.0 119.9 jit_solution(7547943514322467768)
XLA Ops:
  0.6 1.6 %copy.17 = s32[8,25,1024]{2,1,0:T(8,128)S(1)} copy(s32[8,25,1024]{2,0,1:T(8,128)} %bitcast.19) | data formatting | bytes 1638400 | tf_op jit(solution)/shard_map/transpose | solution.py:523
  2.3 0.0 copy-start.5
  2.3 0.0 copy-start
  2.3 0.1 reshape.29.nbr_ref
  2.4 0.8 copy-done.5
  3.2 0.3 copy-done
  3.5 0.0 copy-start.3
  3.5 49.8 %neighbour_sums.1 = (bf16[8,192,128]{2,1,0:T(8,128)(2,1)S(1)}, bf16[192,128]{1,0:T(8,128)(2,1)S(1)}, f32[8,128]{1,0:T(8,128)S(1)}) custom-call(bf16[24,16384]{1,0:T(8,128)(2,1)S(1)} %copy-done, s32[33792]{0:T(1024)S(1)} %concatenate.9.front_ref, s32[1600,128]{1,0:T(8,128)S(1)} %reshape.29.nbr_ref), custom_call_target="tpu_custom_call" | custom-call | flops 200000000 | bytes 100000000 | tf_op jit(solution)/shard_map/neighbour_sums/pallas_call | solution.py:210
  53.2 0.0 copy-done.3
  53.3 0.0 copy-start.4
  53.3 0.1 copy.18
  53.4 0.8 copy-done.4
  54.2 0.0 copy-start.6
  54.2 0.0 copy-start.7
  54.2 0.1 copy.19
  54.3 0.6 copy-done.6
  54.9 0.0 copy-done.7
  54.9 0.0 copy-start.9
  54.9 0.7 copy-done.9
  55.6 0.0 copy-start.8
  55.6 0.7 copy-done.8
  56.3 0.1 pad_maximum_fusion.1.side_ref
  56.4 0.0 copy-start.1
  56.4 0.0 copy-start.2
  56.4 0.7 copy-done.1
  57.1 0.0 copy-done.2
  57.1 60.1 %layers.1 = (f32[8,153]{1,0:T(8,128)S(1)}, bf16[8,4,16,306]{3,2,1,0:T(8,128)(2,1)S(1)}) custom-call(bf16[8,192,128]{2,1,0:T(8,128)(2,1)S(1)} %get-tuple-element.8.part_ref, bf16[192,128]{1,0:T(8,128)(2,1)S(1)} %get-tuple-element.9.self_ref, f32[8,128]{1,0:T(8,128)S(1)} %get-tuple-element.10.deg_ref, bf16[48,512]{1,0:T(8,128)(2,1)S(1)} %pad_maximum_fusion.w_ref, ...), custom_call_target="tpu_custom_call" | custom-call | flops 300000000 | bytes 10000000 | tf_op jit(solution)/shard_map/layers/pallas_call | solution.py:473
  117.2 0.1 convert_bitcast_fusion
  117.3 0.1 copy.20
  117.3 0.2 fusion
  117.5 0.9 copy.21
  118.4 0.9 copy.22
  119.3 0.6 copy.24
  (3 shorter events, 0.0 us)
Async XLA Ops:
  2.3 0.9 copy-start.5
  2.3 1.2 %copy-start = (bf16[24,16384]{1,0:T(8,128)(2,1)S(1)}, bf16[24,16384]{1,0:T(8,128)(2,1)}, u32[]{:S(2)}) copy-start(bf16[24,16384]{1,0:T(8,128)(2,1)} %feats_ref.1) | copy-start | bytes 2359300
  3.5 49.8 %copy-start.3 = (bf16[512,153]{0,1:T(8,128)(2,1)S(1)}, bf16[512,153]{0,1:T(8,128)(2,1)}, u32[]{:S(2)}) copy-start(bf16[512,153]{0,1:T(8,128)(2,1)} %param.18) | copy-start | bytes 470020
  53.3 0.9 copy-start.4
  54.2 0.7 copy-start.6
  54.2 0.8 copy-start.7
  54.9 0.7 copy-start.9
  55.6 0.7 copy-start.8
  56.4 0.7 copy-start.1
  56.4 0.7 copy-start.2

commit v3 on v2

v3 whole, which is shorter than its diff:
```python
import functools

import jax
import jax.numpy as jnp
from jax import lax
from jax.experimental import pallas as pl
from jax.experimental.pallas import tpu as pltpu
from jax.sharding import PartitionSpec as P

LANES = 128
UNROLL = 4
BLOCK = 8
CHUNK = 32
CLASSES = 160
FAN2 = 15
DENSE = 8
WORD_BITS = 15
WORD = 1 << WORD_BITS
MESH = pl.DeviceIdType.MESH
F32 = jnp.float32
BF16 = jnp.bfloat16
VALID = 1 << 29
RANK_AT = 18


def aligned(index, size):
    return pl.ds(pl.multiple_of(index * size, size), size)


def gather_kernel(
    nb, feats_ref, front_ref, ids_ref, nbr_ref, wn_ref, ws_ref, dl_ref, second_ref,
    out_ref, self_ref, deg_ref, w_ref, side_ref,
    table, acc, own, one, two, pairs_v, lists_v, pairs_s, lists_s, front_s, sems, front_sem, pair_sem,
):
    width = feats_ref.shape[0]
    verts = feats_ref.shape[1]
    fan = nbr_ref.shape[0]
    per = fan * nb
    total = per * 8
    targets = 8 * LANES
    fs = front_ref.shape[0] // nb
    fs_bits = fs.bit_length() - 1
    graph = lax.axis_index("graph")

    fetch = pltpu.make_async_copy(front_ref, front_s, front_sem)
    fetch.start()

    def turn(i, c):
        block = feats_ref[:, aligned(i, LANES)].astype(F32)
        table[aligned(i, LANES), 0:width] = block.T
        return c

    lax.fori_loop(0, verts // LANES, turn, 0, unroll=4)
    table[verts : verts + 8, :] = jnp.zeros((8, LANES), F32)

    acc[nb * targets : nb * targets + 8, :] = jnp.zeros((8, LANES), F32)

    w_ref[...] = jnp.concatenate(
        [wn_ref[...].astype(F32), ws_ref[...].astype(F32)], axis=0
    ).astype(BF16)
    side_ref[...] = jnp.zeros_like(side_ref)
    side_ref[:, 0 : dl_ref.shape[1]] = dl_ref[...]
    side_ref[:, CLASSES : CLASSES + second_ref.shape[1]] = second_ref[...].astype(F32)
    degree = jnp.zeros((1, targets), F32)
    for k in range(fan):
        degree = degree + jnp.where(nbr_ref[k, pl.ds(graph, 1), :] >= 0, 1.0, 0.0)
    deg_ref[...] = degree

    part = (nb, targets)
    start = lax.broadcasted_iota(jnp.int32, part, 0) * fs
    tile = lax.broadcasted_iota(jnp.int32, part, 1) >> 7
    seen = jnp.zeros(part, jnp.int32)
    pair = [jnp.zeros(part, jnp.int32), jnp.zeros(part, jnp.int32)]
    for k in range(fan):
        ids = nbr_ref[k]
        here = (ids >> fs_bits) == graph
        local = ids & (fs - 1)
        for j in range(2):
            pair[j] = jnp.where(here & (seen == j), local, pair[j])
        entry = jnp.where(here & (seen > 1), VALID + (local + start) * 8 + tile, 0)
        for q in range(8):
            one[q * per + k * nb : q * per + (k + 1) * nb, :] = entry[
                :, q * LANES : (q + 1) * LANES
            ]
        seen = seen + jnp.where(here, 1, 0)
    for q in range(8):
        cut = slice(q * LANES, (q + 1) * LANES)
        found = [jnp.zeros((nb, LANES), jnp.int32), jnp.zeros((nb, LANES), jnp.int32)]
        for k in range(fs // LANES):
            line = ids_ref[:, k * LANES : (k + 1) * LANES]
            for j in range(2):
                at = pair[j][:, cut]
                got = jnp.take_along_axis(line, at & (LANES - 1), axis=1)
                found[j] = jnp.where((at >> 7) == k, got, found[j])
        for j in range(2):
            found[j] = jnp.where(seen[:, cut] > j, found[j], verts)
        pairs_v[q * nb : (q + 1) * nb, :] = found[1] * WORD + found[0]
    pairs = pltpu.make_async_copy(pairs_v, pairs_s, pair_sem)
    pairs.start()

    below = (
        lax.broadcasted_iota(jnp.int32, (per, per), 0)
        > lax.broadcasted_iota(jnp.int32, (per, per), 1)
    ).astype(F32).astype(BF16)
    lost = jnp.zeros((1, LANES), jnp.int32)
    for q in range(8):
        entry = one[q * per : (q + 1) * per, :]
        gone = jnp.where(entry == 0, 1.0, 0.0)
        before = jnp.dot(below, gone.astype(BF16), preferred_element_type=F32)
        rank = before.astype(jnp.int32) + lost
        one[q * per : (q + 1) * per, :] = jnp.where(entry == 0, 0, entry + rank * (1 << RANK_AT))
        lost = lost + jnp.sum(gone, axis=0, keepdims=True).astype(jnp.int32)
    count = total - lost

    src, dst = one, two
    bits = (total - 1).bit_length()
    block = 64
    for step in range(bits):
        far = 1 << step
        flag = 1 << (RANK_AT + step)
        for at in range(0, total, block):
            stay = src[at : at + block, :]
            have = max(0, min(block, total - at - far))
            kept = jnp.where((stay & flag) != 0, 0, stay)
            if have > 0:
                move = src[at + far : at + far + have, :]
                if have < block:
                    move = jnp.concatenate(
                        [move, jnp.zeros((block - have, LANES), jnp.int32)], axis=0
                    )
                kept = jnp.where((move & flag) != 0, move, kept)
            dst[at : at + block, :] = kept
        src, dst = dst, src

    lane_row = lax.broadcasted_iota(jnp.int32, (LANES, LANES), 1)
    key_row = jnp.broadcast_to(count * LANES, (LANES, LANES)) + lane_row
    key_col = key_row.astype(F32).T
    ahead = jnp.where(key_row.astype(F32) > key_col, 1.0, 0.0)
    place = jnp.sum(ahead, axis=1, keepdims=True).astype(jnp.int32)
    order = jnp.where(place == lane_row, 1.0, 0.0).astype(BF16)

    def shuffle(values):
        got = jnp.dot(values.astype(F32).astype(BF16), order, preferred_element_type=F32)
        return got.astype(jnp.int32)

    wide = jnp.broadcast_to(count, (8, LANES))
    sorted_count = (shuffle(wide // 64) * 64 + shuffle(wide % 64))[0:1]
    lane_id = shuffle(lax.broadcasted_iota(jnp.int32, (8, LANES), 1))[0:1]
    count_col = jnp.broadcast_to(sorted_count.astype(F32), (LANES, LANES)).T
    deepest = jnp.max(count)
    chunks = (deepest + CHUNK - 1) // CHUNK

    def prepare(ch, slot):
        entries = src[aligned(ch, CHUNK), :]
        ident = (entries >> 3) & (nb * fs - 1)
        ident = shuffle(ident >> 8) * 256 + shuffle(ident & 255)
        group = shuffle(entries & 7)
        at_row = ch * CHUNK + lax.broadcasted_iota(jnp.int32, (CHUNK, LANES), 0)
        live = sorted_count > at_row
        goal = (ident >> fs_bits) * targets + group * LANES + lane_id
        word = jnp.where(live, goal * WORD + ident, nb * targets * WORD)
        lists_v[slot, 0:CHUNK, :] = word
        row_at = (ch * CHUNK + lane_row).astype(F32)
        in_row = jnp.sum(jnp.where(count_col > row_at, 1.0, 0.0), axis=0, keepdims=True)
        groups = (in_row.astype(jnp.int32) + (UNROLL - 1)) // UNROLL
        lists_v[slot, CHUNK : CHUNK + 8, :] = jnp.broadcast_to(groups, (8, LANES))

    def transfer(slot):
        return pltpu.make_async_copy(
            lists_v.at[slot],
            lists_s.at[pl.ds(pl.multiple_of(slot * (CHUNK + 8), 8), CHUNK + 8)],
            sems.at[slot],
        )

    @pl.when(chunks > 0)
    def _():
        prepare(0, 0)
        transfer(0).start()

    fetch.wait()
    pairs.wait()

    def dense(r, c):
        base = (r & (nb - 1)) * targets + (r >> (nb.bit_length() - 1)) * LANES
        for at in range(0, LANES, DENSE):
            words = [pairs_s[r, at + u] for u in range(DENSE)]
            got = [
                table[pl.ds(w & (WORD - 1), 1), :] + table[pl.ds(w >> WORD_BITS, 1), :]
                for w in words
            ]
            for u in range(DENSE):
                acc[pl.ds(pl.multiple_of(base, LANES) + at + u, 1), :] = got[u]
        return c

    lax.fori_loop(0, nb * 8, dense, 0)

    def chunk(ch, c):
        slot = ch & 1
        base = slot * (CHUNK + 8)
        transfer(slot).wait()

        @pl.when(ch + 1 < chunks)
        def _():
            prepare(ch + 1, 1 - slot)
            transfer(1 - slot).start()

        def row(r, c):
            def group(g):
                words = [lists_s[at, g * UNROLL + u] for u in range(UNROLL)]
                got = [table[pl.ds(front_s[w & (WORD - 1)], 1), :] for w in words]
                goals = [w >> WORD_BITS for w in words]
                old = [acc[pl.ds(a, 1), :] for a in goals]
                for u in range(UNROLL):
                    acc[pl.ds(goals[u], 1), :] = got[u] + old[u]

            groups = lists_s[base + CHUNK, r]
            at = base + r

            def block(h):
                for g in range(h * BLOCK, (h + 1) * BLOCK):
                    group(g)

            for h in range(LANES // UNROLL // BLOCK):
                pl.when(h * BLOCK < groups)(functools.partial(block, h))
            return c

        return lax.fori_loop(0, jnp.minimum(CHUNK, deepest - ch * CHUNK), row, c)

    lax.fori_loop(0, chunks, chunk, 0)

    def mine(i, c):
        base = graph * fs + i * UNROLL
        got = [table[pl.ds(front_s[base + u], 1), :] for u in range(UNROLL)]
        for u in range(UNROLL):
            own[pl.ds(i * UNROLL + u, 1), :] = got[u]
        return c

    lax.fori_loop(0, targets // UNROLL, mine, 0)

    for b in range(nb):
        turned = [
            acc[b * targets + q * LANES : b * targets + (q + 1) * LANES, 0:width].T
            for q in range(8)
        ]
        out_ref[b] = jnp.concatenate(turned, axis=0).astype(BF16)
    for q in range(8):
        self_ref[q] = own[q * LANES : (q + 1) * LANES, 0:width].T


def gather(feats, front, ids, nbr, wn, ws, dl, second, nb):
    width, verts = feats.shape
    total = nbr.shape[0] * nb * 8
    vmem = pl.BlockSpec(memory_space=pltpu.VMEM)
    return pl.pallas_call(
        functools.partial(gather_kernel, nb),
        out_shape=(
            jax.ShapeDtypeStruct((nb, 8 * width, LANES), BF16),
            jax.ShapeDtypeStruct((8, width, LANES), F32),
            jax.ShapeDtypeStruct((1, 8 * LANES), F32),
            jax.ShapeDtypeStruct((2 * width, wn.shape[1]), BF16),
            jax.ShapeDtypeStruct((8, CLASSES + 16), F32),
        ),
        in_specs=[vmem, pl.BlockSpec(memory_space=pl.ANY)] + [vmem] * 6,
        out_specs=(vmem,) * 5,
        scratch_shapes=[
            pltpu.VMEM((verts + 8, LANES), F32),
            pltpu.VMEM((nb * 8 * LANES + 8, LANES), F32),
            pltpu.VMEM((8 * LANES, LANES), F32),
            pltpu.VMEM((total + 64, LANES), jnp.int32),
            pltpu.VMEM((total + 64, LANES), jnp.int32),
            pltpu.VMEM((nb * 8, LANES), jnp.int32),
            pltpu.VMEM((2, CHUNK + 8, LANES), jnp.int32),
            pltpu.SMEM((nb * 8, LANES), jnp.int32),
            pltpu.SMEM((2 * (CHUNK + 8), LANES), jnp.int32),
            pltpu.SMEM(front.shape, jnp.int32),
            pltpu.SemaphoreType.DMA((2,)),
            pltpu.SemaphoreType.DMA,
            pltpu.SemaphoreType.DMA,
        ],
        compiler_params=pltpu.CompilerParams(vmem_limit_bytes=40 * 1024 * 1024),
        cost_estimate=pl.CostEstimate(flops=200000000, bytes_accessed=100000000, transcendentals=0),
        name="neighbour_sums",
    )(feats, front, ids, nbr, wn, ws, dl, second)


def split_dot(ones, wide, dims):
    high = wide.astype(BF16)
    low = (wide - high.astype(F32)).astype(BF16)
    return lax.dot_general(ones, high, dims, preferred_element_type=F32) + lax.dot_general(
        ones, low, dims, preferred_element_type=F32
    )


NN = (((1,), (0,)), ((), ()))
TN = (((0,), (0,)), ((), ()))
NT = (((1,), (1,)), ((), ()))


def layers_kernel(
    nz, ny,
    part_ref, self_ref, deg_ref, w_ref, side_ref, b1_ref, w2s_ref, w2n_ref, b2_ref,
    logits_ref, gs_ref, gn_ref,
    grads_ref, gotw, sv, sall, got1, xs, got2, pre, got3, lp, got4, l2, got5,
    gp, gotg, gz, gotz, gall, gy,
    sw, rw, sf, rf, sa, ra, sb, rb, s0, r0, s1, r1, s2, r2, s3, r3, s4, r4, s5, r5,
    sg, rg, sz, rz, sq, rq, sy, ry, sx, rx, sh, rh,
):
    feat = lax.axis_index("feat")
    graph = lax.axis_index("graph")
    ng = part_ref.shape[0]
    z = feat // ny
    y = feat % ny
    core = graph % 2
    width = part_ref.shape[1] // 8
    cdim = w2s_ref.shape[0]
    rows = 2 * CLASSES // ng
    bit = rows // nz

    def at_graph(d):
        return (feat, (graph + d) % ng)

    def at_z(d):
        return (((z + d) % nz) * ny + y, graph)

    def at_y(d):
        return (z * ny + (y + d) % ny, graph)

    sibling = (feat, graph + 1 - 2 * core)

    barrier = pltpu.get_barrier_semaphore()
    for d in range(1, ng):
        pl.semaphore_signal(barrier, inc=1, device_id=at_graph(d), device_id_type=MESH)
    for d in range(1, nz):
        pl.semaphore_signal(barrier, inc=1, device_id=at_z(d), device_id_type=MESH)
    for d in range(1, ny):
        pl.semaphore_signal(barrier, inc=1, device_id=at_y(d), device_id_type=MESH)
    pl.semaphore_wait(barrier, (ng - 1) + (nz - 1) + (ny - 1))

    def remote(src, dst, ssem, rsem, where):
        return pltpu.make_async_remote_copy(
            src_ref=src, dst_ref=dst, send_sem=ssem, recv_sem=rsem,
            device_id=where, device_id_type=MESH,
        )

    def send(src, dst, ssem, rsem, where):
        copy = remote(src, dst, ssem, rsem, where)
        copy.start()
        return copy

    c1 = [
        send(part_ref.at[(graph + d) % ng], got1.at[d], s1.at[d], r1.at[d], at_graph(d))
        for d in range(1, ng)
    ]
    ca = [send(side_ref, sv.at[z], sa.at[d], ra.at[d], at_z(d)) for d in range(1, nz)]

    def weight_copy(d):
        return remote(w_ref, gotw.at[z], sw.at[d], rw.at[d], at_z(d))

    def weight_pass(d):
        block = gotw.at[(z - d + nz) % nz]
        return remote(block, block, sf.at[d], rf.at[d], sibling)

    @pl.when(z % 2 == core)
    def _():
        for d in range(1, nz):
            weight_copy(d).start()

    c0 = [
        send(
            self_ref.at[(z + d) % nz], got2.at[z, pl.ds(width, width)],
            s0.at[d], r0.at[d], at_z(d),
        )
        for d in range(1, nz)
    ]
    gotw[z] = w_ref[...]
    sv[z] = side_ref[...]
    got2[z, width : 2 * width, :] = self_ref[z]

    for c in ca:
        c.wait_recv()
    cb = [send(sv, sall.at[y], sb.at[d], rb.at[d], at_y(d)) for d in range(1, ny)]
    sall[y] = sv[...]

    summed = part_ref[graph].astype(F32)
    for d in range(1, ng):
        c1[d - 1].wait_recv()
        summed = summed + got1[d].astype(F32)
    for q in range(8):
        xs[q] = summed[q * width : (q + 1) * width] / deg_ref[:, q * LANES : (q + 1) * LANES]
    c2 = [
        send(
            xs.at[(z + d) % nz], got2.at[z, pl.ds(0, width)], s2.at[d], r2.at[d], at_z(d)
        )
        for d in range(1, nz)
    ]
    got2[z, 0:width, :] = xs[z]

    for d in range(1, nz):
        @pl.when((z + d) % 2 == core)
        def _():
            weight_copy(d).wait_recv()
            weight_pass(d).start()

    for c in cb:
        c.wait_recv()
    seeds = ny * nz * 8
    side = sall[...].reshape(seeds, side_ref.shape[1])
    dl = side[:, :CLASSES]
    second = side[:, CLASSES:].astype(jnp.int32)
    taken = lax.broadcasted_iota(jnp.int32, second.shape, 1) < FAN2
    deg2 = jnp.sum(jnp.where((second >= 0) & taken, 1.0, 0.0), axis=1, keepdims=True)
    spot = z * LANES + lax.broadcasted_iota(jnp.int32, (seeds, LANES), 1)
    hits = jnp.zeros((seeds, LANES), F32)
    for k in range(FAN2):
        hits = hits + jnp.where(second[:, k : k + 1] == spot, 1.0, 0.0)
    hits = hits.astype(BF16)
    at = lax.broadcasted_iota(jnp.int32, (seeds, LANES), 0)
    row = ((at // 8) % nz) * (ny * 8) + (at // (8 * nz)) * 8 + at % 8
    same = jnp.where(row == spot, 1.0, 0.0).astype(BF16)

    for c in c0 + c2:
        c.wait_recv()
    x = got2[...].reshape(nz * 2 * width, LANES)
    for d in range(1, nz):
        @pl.when((z + d) % 2 != core)
        def _():
            weight_pass(d).wait_recv()
    w = gotw[...].reshape(nz * 2 * width, w_ref.shape[1])
    high = x.astype(BF16)
    low = (x - high.astype(F32)).astype(BF16)
    part = lax.dot_general(high, w, TN, preferred_element_type=F32) + lax.dot_general(
        low, w, TN, preferred_element_type=F32
    )
    for k in range(ny):
        pre[k] = part[:, k * LANES : (k + 1) * LANES]
    c3 = [
        send(pre.at[(y + d) % ny], got3.at[d], s3.at[d], r3.at[d], at_y(d)) for d in range(1, ny)
    ]

    def exact(wide, ones):
        total = jnp.zeros((wide.shape[1], ones.shape[1]), F32)
        for _ in range(3):
            piece = wide.astype(BF16)
            total = total + lax.dot_general(piece, ones, TN, preferred_element_type=F32)
            wide = wide - piece.astype(F32)
        return total

    cot = jnp.concatenate([exact(dl, same), exact(dl / deg2, hits)], axis=0)
    cot_high = cot.astype(BF16)
    cot_low = (cot - cot_high.astype(F32)).astype(BF16)

    h = pre[y] + b1_ref[y]
    for d in range(1, ny):
        c3[d - 1].wait_recv()
        h = h + got3[d]
    h = jnp.maximum(h, 0.0).astype(BF16)

    g = jnp.dot(cot_high, h, preferred_element_type=F32) + jnp.dot(
        cot_low, h, preferred_element_type=F32
    )
    gp[...] = g.reshape(ng, rows, LANES)
    cg = [
        send(gp.at[(graph + d) % ng], gotg.at[d], sg.at[d], rg.at[d], at_graph(d))
        for d in range(1, ng)
    ]

    columns = pl.ds(pl.multiple_of(y * LANES, LANES), LANES)
    zs = lax.dot_general(h, w2s_ref[:, columns], NT, preferred_element_type=F32)
    zn = lax.dot_general(h, w2n_ref[:, columns], NT, preferred_element_type=F32)

    gsum = gp[graph]
    for d in range(1, ng):
        cg[d - 1].wait_recv()
        gsum = gsum + gotg[d]
    for k in range(nz):
        gz[k] = gsum[k * bit : (k + 1) * bit]
    cz = [send(gz.at[(z + d) % nz], gotz.at[d], sz.at[d], rz.at[d], at_z(d)) for d in range(1, nz)]

    scores = split_dot(hits, zn, NN) / deg2 + split_dot(same, zs, NN)
    lp[...] = scores.reshape(ny, nz, 8, cdim)
    c4 = [
        send(lp.at[(y + d) % ny], got4.at[d], s4.at[d], r4.at[d], at_y(d)) for d in range(1, ny)
    ]

    whole = gz[z]
    for d in range(1, nz):
        cz[d - 1].wait_recv()
        whole = whole + gotz[d]
    gall[z] = whole
    cq = [send(gall.at[z], gall.at[z], sq.at[d], rq.at[d], at_z(d)) for d in range(1, nz)]

    lsum = lp[y]
    for d in range(1, ny):
        c4[d - 1].wait_recv()
        lsum = lsum + got4[d]
    l2[...] = lsum
    c5 = [
        send(l2.at[(z + d) % nz], got5.at[d], s5.at[d], r5.at[d], at_z(d)) for d in range(1, nz)
    ]

    for c in cq:
        c.wait_recv()
    gy[y] = jnp.concatenate([gall[k] for k in range(nz)], axis=0)
    cy = [send(gy.at[y], gy.at[y], sy.at[d], ry.at[d], at_y(d)) for d in range(1, ny)]
    for c in cy:
        c.wait_recv()
    grads_ref[graph] = gy[...].reshape(ny * rows, LANES).astype(BF16)
    mine = grads_ref.at[graph]
    cx = [send(mine, mine, sx.at[d], rx.at[d], at_graph(2 * d)) for d in range(1, ng // 2)]
    ch = [send(mine, mine, sh.at[0], rh.at[0], sibling)]

    final = l2[z] + b2_ref[...]
    for d in range(1, nz):
        c5[d - 1].wait_recv()
        final = final + got5[d]
    logits_ref[...] = final

    for d in range(1, ng // 2):
        cx[d - 1].wait_recv()
        block = grads_ref.at[(graph + ng - 2 * d) % ng]
        ch.append(send(block, block, sh.at[d], rh.at[d], sibling))
    for c in ch:
        c.wait_recv()
    half = ng // 2
    for k in range(ng):
        out = gs_ref if k < half else gn_ref
        base = (k % half) * rows
        keep = min(rows, cdim - base)
        block = grads_ref[k].astype(F32)
        for j in range(ny):
            out[base : base + keep, j * LANES : (j + 1) * LANES] = block[
                j * rows : j * rows + keep
            ]
    for c in ca + cb + c0 + c1 + c2 + c3 + cg + c4 + cz + cq + c5 + cy + cx + ch:
        c.wait_send()

    @pl.when(z % 2 == core)
    def _():
        for d in range(1, nz):
            weight_copy(d).wait_send()

    for d in range(1, nz):
        @pl.when((z + d) % 2 == core)
        def _():
            weight_pass(d).wait_send()


def layers(nz, ny, part, own, deg, w, side, b1, w2s, w2n, b2):
    ng, rows, _ = part.shape
    width = rows // 8
    cdim = w2s.shape[0]
    cut = 2 * CLASSES // ng
    vmem = pl.BlockSpec(memory_space=pltpu.VMEM)
    dma = lambda n: pltpu.SemaphoreType.DMA((n,))
    pair = lambda n: [dma(n), dma(n)]
    return pl.pallas_call(
        functools.partial(layers_kernel, nz, ny),
        out_shape=(
            jax.ShapeDtypeStruct((8, cdim), F32),
            jax.ShapeDtypeStruct(w2s.shape, F32),
            jax.ShapeDtypeStruct(w2n.shape, F32),
        ),
        in_specs=[vmem] * 9,
        out_specs=(vmem, vmem, vmem),
        scratch_shapes=[
            pltpu.VMEM((ng, ny * cut, LANES), BF16),
            pltpu.VMEM((nz, 2 * width, w.shape[1]), BF16),
            pltpu.VMEM((nz,) + side.shape, F32),
            pltpu.VMEM((ny, nz) + side.shape, F32),
            pltpu.VMEM((ng, rows, LANES), BF16),
            pltpu.VMEM((8, width, LANES), F32),
            pltpu.VMEM((nz, 2 * width, LANES), F32),
            pltpu.VMEM((ny, LANES, LANES), F32),
            pltpu.VMEM((ny, LANES, LANES), F32),
            pltpu.VMEM((ny, nz, 8, cdim), F32),
            pltpu.VMEM((ny, nz, 8, cdim), F32),
            pltpu.VMEM((nz, 8, cdim), F32),
            pltpu.VMEM((nz, 8, cdim), F32),
            pltpu.VMEM((ng, cut, LANES), F32),
            pltpu.VMEM((ng, cut, LANES), F32),
            pltpu.VMEM((nz, cut // nz, LANES), F32),
            pltpu.VMEM((nz, cut // nz, LANES), F32),
            pltpu.VMEM((nz, cut // nz, LANES), F32),
            pltpu.VMEM((ny, cut, LANES), F32),
        ]
        + pair(nz) + pair(nz) + pair(nz) + pair(ny) + pair(nz) + pair(ng) + pair(nz)
        + pair(ny) + pair(ny) + pair(nz) + pair(ng) + pair(nz) + pair(nz) + pair(ny)
        + pair(ng) + pair(ng),
        compiler_params=pltpu.CompilerParams(
            collective_id=0, has_side_effects=True, vmem_limit_bytes=40 * 1024 * 1024
        ),
        cost_estimate=pl.CostEstimate(flops=300000000, bytes_accessed=10000000, transcendentals=0),
        name="layers",
    )(part, own, deg, w, side, b1, w2s, w2n, b2)


def on_device(feats, front_ids, nbr1, nbr2, w1_self, w1_neigh, b1, w2_self, w2_neigh, b2, dlogits):
    nb, targets, fan = nbr1.shape
    width, verts = feats.shape
    hidden, cdim = w2_self.shape
    nz, ny = 8, 4

    part, own, deg, w, side = gather(
        feats, front_ids.reshape(-1), front_ids[:, 0, :], nbr1.transpose(2, 0, 1),
        w1_neigh, w1_self,
        dlogits[0], nbr2[0], nb,
    )
    logits, grad_s, grad_n = layers(
        nz, ny, part, own, deg, w, side,
        b1.reshape(ny, 1, LANES), w2_self.T, w2_neigh.T, b2.reshape(1, cdim),
    )
    return (logits[None], grad_s.T, grad_n.T)


def solution(mesh):
    in_specs = (
        P("feat", "graph"),
        P(None, "graph", None),
        P(),
        P("graph", "feat", None),
        P("feat", None),
        P("feat", None),
        P(),
        P(),
        P(),
        P(),
        P("graph", "feat", None),
    )
    out_specs = (P("graph", "feat", None), P(), P())
    return jax.shard_map(
        on_device, mesh=mesh, in_specs=in_specs, out_specs=out_specs, check_vma=False
    )
```

time: 120 us -> 94.8 us (0.79)
  Pallas kernels: 110 us -> 87.7 us
  local copies, waits for them, and re-layouts: 9.2 us -> 6.07 us
    pallas_call x1, Pallas kernels: 49.8 us -> 33.7 us  [gather(): pl.pallas_call(functools.partial(gather_kernel, nb), out_shape=(jax.Shape...]
    pallas_call x1, Pallas kernels: 60.1 us -> 54 us  [layers(): pl.pallas_call(functools.partial(layers_kernel, nz, ny), out_shape=(jax.S...]
    transpose x1 -> x0, local copies, waits for them, and re-layouts: 1.63 us -> none  [on_device(): turned = nbr1.transpose(0, 2, 1)]
    unnamed x25 -> x26, local copies, waits for them, and re-layouts: 7.18 us -> 6.07 us
where the time goes in v3:
time: 94.8 us; the launch traced here: 94.6 us
  Pallas kernels  87.7 us (93%)
  local copies, waits for them, and re-layouts  6.07 us (6%)
    pallas_call x1, Pallas kernels, layers(): pl.pallas_call(functools.partial(layers_kernel, nz, ny), out_shape=(jax.S...  54 us
    pallas_call x1, Pallas kernels, gather(): pl.pallas_call(functools.partial(gather_kernel, nb), out_shape=(jax.Shape...  33.7 us
    unnamed x26, local copies, waits for them, and re-layouts  6.07 us

profile of v3, /device:TPU:1, one launch (start us, length us, event | category | flops | bytes accessed | tf_op | source)
XLA Modules:
  0.0 94.6 jit_solution(15211112683389034652)
XLA Ops:
  0.6 0.0 copy-start.2
  0.6 0.0 copy-start.3
  0.7 0.0 copy-start.4
  0.7 0.0 copy-start.5
  0.7 0.0 copy-start.6
  0.7 1.1 %copy.16 = s32[8,1,4096]{2,0,1:T(8,128)S(1)} copy(s32[8,1,4096]{2,1,0:T(1,128)} %param.12) | data formatting | bytes 262144
  1.7 0.0 copy-done.2
  1.8 0.0 copy-done.3
  1.8 0.0 copy-done.4
  1.8 0.0 copy-done.5
  1.8 0.0 copy-done.6
  1.8 0.0 copy-start
  1.8 1.1 %copy-done = s32[8,1024,25]{1,0,2:T(8,128)S(1)} copy-done((s32[8,1024,25]{1,0,2:T(8,128)S(1)}, s32[8,1024,25]{1,0,2:T(8,128)}, u32[]{:S(2)}) %copy-start) | copy-done | bytes 819224
  2.9 0.0 copy-start.1
  2.9 1.1 %copy-done.1 = bf16[24,16384]{1,0:T(8,128)(2,1)S(1)} copy-done((bf16[24,16384]{1,0:T(8,128)(2,1)S(1)}, bf16[24,16384]{1,0:T(8,128)(2,1)}, u32[]{:S(2)}) %copy-start.1) | copy-done | bytes 786456
  4.1 0.0 copy-start.7
  4.1 0.0 copy-start.8
  4.1 33.7 %neighbour_sums.1 = (bf16[8,192,128]{2,1,0:T(8,128)(2,1)S(1)}, f32[8,24,128]{2,1,0:T(8,128)S(1)}, f32[1,1024]{1,0:T(1,128)S(1)}, bf16[48,512]{1,0:T(8,128)(2,1)S(1)}, f32[8,176]{1,0:T(8,128)S(1)}) custom-call(bf16[24,16384]{1,0:T(8,128)(2,1)S(1)} %copy-done.1, s32[32768]{0:T(1024)S(1)} %bitcast.15, s32[8,4096]{1,0:T(8,128)S(1)} %bitcast.16, ...), custom_call_target="tpu_custom_call" | custom-call | flops 200000000 | bytes 100000000 | tf_op jit(solution)/shard_map/neighbour_sums/pallas_call | solution.py:254
  37.8 0.0 copy-start.9
  37.8 0.0 copy-start.10
  37.8 0.0 copy-done.7
  37.8 0.0 copy-done.8
  37.9 0.6 copy-done.9
  38.5 0.0 copy-done.10
  38.5 54.0 %layers.1 = (f32[8,153]{1,0:T(8,128)S(1)}, f32[153,512]{1,0:T(8,128)S(1)}, f32[153,512]{1,0:T(8,128)S(1)}) custom-call(bf16[8,192,128]{2,1,0:T(8,128)(2,1)S(1)} %get-tuple-element.11.part_ref, f32[8,24,128]{2,1,0:T(8,128)S(1)} %get-tuple-element.12.self_ref, f32[1,1024]{1,0:T(1,128)S(1)} %get-tuple-element.13.deg_ref, ...), custom_call_target="tpu_custom_call" | custom-call | flops 300000000 | bytes 10000000 | tf_op jit(solution)/shard_map/layers/pallas_call | solution.py:556
  92.5 0.6 copy.20
  93.1 0.7 copy.21
  93.8 0.7 copy.22
Async XLA Ops:
  0.6 1.1 %copy-start.2 = (s32[8,1,4096]{2,1,0:T(1,128)S(1)}, s32[8,1,4096]{2,1,0:T(1,128)}, u32[]{:S(2)}) copy-start(s32[8,1,4096]{2,1,0:T(1,128)} %param.12) | copy-start | bytes 393220
  0.6 1.1 %copy-start.3 = (bf16[24,512]{1,0:T(8,128)(2,1)S(1)}, bf16[24,512]{1,0:T(8,128)(2,1)}, u32[]{:S(2)}) copy-start(bf16[24,512]{1,0:T(8,128)(2,1)} %wn_ref.1) | copy-start | bytes 73732
  0.7 1.1 %copy-start.4 = (bf16[24,512]{1,0:T(8,128)(2,1)S(1)}, bf16[24,512]{1,0:T(8,128)(2,1)}, u32[]{:S(2)}) copy-start(bf16[24,512]{1,0:T(8,128)(2,1)} %ws_ref.1) | copy-start | bytes 73732
  0.7 1.1 %copy-start.5 = (f32[1,8,153]{2,1,0:T(8,128)S(1)}, f32[1,8,153]{2,1,0:T(8,128)}, u32[]{:S(2)}) copy-start(f32[1,8,153]{2,1,0:T(8,128)} %param.21) | copy-start | bytes 14692
  0.7 1.1 %copy-start.6 = (s32[1,8,15]{2,1,0:T(8,128)S(1)}, s32[1,8,15]{2,1,0:T(8,128)}, u32[]{:S(2)}) copy-start(s32[1,8,15]{2,1,0:T(8,128)} %param.14) | copy-start | bytes 1444
  1.8 1.1 %copy-start = (s32[8,1024,25]{1,0,2:T(8,128)S(1)}, s32[8,1024,25]{1,0,2:T(8,128)}, u32[]{:S(2)}) copy-start(s32[8,1024,25]{1,0,2:T(8,128)} %param.13) | copy-start | bytes 2457604
  2.9 1.1 %copy-start.1 = (bf16[24,16384]{1,0:T(8,128)(2,1)S(1)}, bf16[24,16384]{1,0:T(8,128)(2,1)}, u32[]{:S(2)}) copy-start(bf16[24,16384]{1,0:T(8,128)(2,1)} %feats_ref.1) | copy-start | bytes 2359300
  4.1 33.8 %copy-start.7 = (bf16[512,153]{0,1:T(8,128)(2,1)S(1)}, bf16[512,153]{0,1:T(8,128)(2,1)}, u32[]{:S(2)}) copy-start(bf16[512,153]{0,1:T(8,128)(2,1)} %param.18) | copy-start | bytes 470020
  4.1 33.8 %copy-start.8 = (bf16[512,153]{0,1:T(8,128)(2,1)S(1)}, bf16[512,153]{0,1:T(8,128)(2,1)}, u32[]{:S(2)}) copy-start(bf16[512,153]{0,1:T(8,128)(2,1)} %param.19) | copy-start | bytes 470020
  37.8 0.7 copy-start.9
  37.8 0.7 copy-start.10

commit v4 on v3

--- a/solution.py
+++ b/solution.py
@@ -12,6 +12,7 @@
 BLOCK = 8
 CHUNK = 32
 CLASSES = 160
+VMEM_BYTES = 60 * 1024 * 1024
 FAN2 = 15
 DENSE = 8
 WORD_BITS = 15
@@ -27,10 +28,23 @@
     return pl.ds(pl.multiple_of(index * size, size), size)
 
 
+def build_table(feats_ref, table):
+    width, verts = feats_ref.shape
+
+    def turn(i, c):
+        block = feats_ref[:, aligned(i, LANES)].astype(F32)
+        table[aligned(i, LANES), 0:width] = block.T
+        return c
+
+    lax.fori_loop(0, verts // LANES, turn, 0, unroll=16)
+    table[verts : verts + 8, :] = jnp.zeros((8, LANES), F32)
+
+
 def gather_kernel(
-    nb, feats_ref, front_ref, ids_ref, nbr_ref, wn_ref, ws_ref, dl_ref, second_ref,
-    out_ref, self_ref, deg_ref, w_ref, side_ref,
-    table, acc, own, one, two, pairs_v, lists_v, pairs_s, lists_s, front_s, sems, front_sem, pair_sem,
+    nb, feats_hbm, front_ref, ids_hbm, nbr_hbm, wn_hbm, ws_hbm, dl_hbm, second_hbm,
+    rest_ref, pairs_v, self_ref, deg_ref, w_ref, side_ref,
+    table, acc, feats_ref, ids_ref, nbr_ref, wn_ref, ws_ref, dl_ref, second_ref, own, one, two, lists_v, lists_s, front_s,
+    sems, front_sem, load_sems,
 ):
     width = feats_ref.shape[0]
     verts = feats_ref.shape[1]
@@ -42,25 +56,24 @@
     fs_bits = fs.bit_length() - 1
     graph = lax.axis_index("graph")
 
+    load_nbr = pltpu.make_async_copy(nbr_hbm, nbr_ref, load_sems.at[0])
+    load_nbr.start()
+    load_ids = pltpu.make_async_copy(ids_hbm, ids_ref, load_sems.at[1])
+    load_ids.start()
+    load_feats = pltpu.make_async_copy(feats_hbm, feats_ref, load_sems.at[2])
+    load_feats.start()
+    small = [
+        pltpu.make_async_copy(a, b, load_sems.at[3 + i])
+        for i, (a, b) in enumerate(
+            [(wn_hbm, wn_ref), (ws_hbm, ws_ref), (dl_hbm, dl_ref), (second_hbm, second_ref)]
+        )
+    ]
+    for load in small:
+        load.start()
     fetch = pltpu.make_async_copy(front_ref, front_s, front_sem)
     fetch.start()
 
-    def turn(i, c):
-        block = feats_ref[:, aligned(i, LANES)].astype(F32)
-        table[aligned(i, LANES), 0:width] = block.T
-        return c
-
-    lax.fori_loop(0, verts // LANES, turn, 0, unroll=4)
-    table[verts : verts + 8, :] = jnp.zeros((8, LANES), F32)
-
-    acc[nb * targets : nb * targets + 8, :] = jnp.zeros((8, LANES), F32)
-
-    w_ref[...] = jnp.concatenate(
-        [wn_ref[...].astype(F32), ws_ref[...].astype(F32)], axis=0
-    ).astype(BF16)
-    side_ref[...] = jnp.zeros_like(side_ref)
-    side_ref[:, 0 : dl_ref.shape[1]] = dl_ref[...]
-    side_ref[:, CLASSES : CLASSES + second_ref.shape[1]] = second_ref[...].astype(F32)
+    load_nbr.wait()
     degree = jnp.zeros((1, targets), F32)
     for k in range(fan):
         degree = degree + jnp.where(nbr_ref[k, pl.ds(graph, 1), :] >= 0, 1.0, 0.0)
@@ -83,20 +96,21 @@
                 :, q * LANES : (q + 1) * LANES
             ]
         seen = seen + jnp.where(here, 1, 0)
+    load_ids.wait()
     for q in range(8):
         cut = slice(q * LANES, (q + 1) * LANES)
         found = [jnp.zeros((nb, LANES), jnp.int32), jnp.zeros((nb, LANES), jnp.int32)]
         for k in range(fs // LANES):
-            line = ids_ref[:, k * LANES : (k + 1) * LANES]
+            line = ids_ref[:, 0, k * LANES : (k + 1) * LANES]
             for j in range(2):
                 at = pair[j][:, cut]
                 got = jnp.take_along_axis(line, at & (LANES - 1), axis=1)
                 found[j] = jnp.where((at >> 7) == k, got, found[j])
         for j in range(2):
             found[j] = jnp.where(seen[:, cut] > j, found[j], verts)
-        pairs_v[q * nb : (q + 1) * nb, :] = found[1] * WORD + found[0]
-    pairs = pltpu.make_async_copy(pairs_v, pairs_s, pair_sem)
-    pairs.start()
+        word = found[1] * WORD + found[0]
+        for b in range(nb):
+            pairs_v[b * 8 + q : b * 8 + q + 1, :] = word[b : b + 1]
 
     below = (
         lax.broadcasted_iota(jnp.int32, (per, per), 0)
@@ -177,22 +191,26 @@
         prepare(0, 0)
         transfer(0).start()
 
+    for load in small:
+        load.wait()
+    w_ref[...] = jnp.concatenate(
+        [wn_ref[...].astype(F32), ws_ref[...].astype(F32)], axis=0
+    ).astype(BF16)
+    side_ref[...] = jnp.zeros_like(side_ref)
+    side_ref[:, 0 : dl_ref.shape[1]] = dl_ref[...]
+    side_ref[:, CLASSES : CLASSES + second_ref.shape[1]] = second_ref[...].astype(F32)
+    load_feats.wait()
+
+    build_table(feats_ref, table)
+
+
+    def clear(i, c):
+        acc[aligned(i, 8), :] = jnp.zeros((8, LANES), F32)
+        return c
+
+    lax.fori_loop(0, acc.shape[0] // 8, clear, 0, unroll=25)
+
     fetch.wait()
-    pairs.wait()
-
-    def dense(r, c):
-        base = (r & (nb - 1)) * targets + (r >> (nb.bit_length() - 1)) * LANES
-        for at in range(0, LANES, DENSE):
-            words = [pairs_s[r, at + u] for u in range(DENSE)]
-            got = [
-                table[pl.ds(w & (WORD - 1), 1), :] + table[pl.ds(w >> WORD_BITS, 1), :]
-                for w in words
-            ]
-            for u in range(DENSE):
-                acc[pl.ds(pl.multiple_of(base, LANES) + at + u, 1), :] = got[u]
-        return c
-
-    lax.fori_loop(0, nb * 8, dense, 0)
 
     def chunk(ch, c):
         slot = ch & 1
@@ -242,7 +260,7 @@
             acc[b * targets + q * LANES : b * targets + (q + 1) * LANES, 0:width].T
             for q in range(8)
         ]
-        out_ref[b] = jnp.concatenate(turned, axis=0).astype(BF16)
+        rest_ref[b] = jnp.concatenate(turned, axis=0)
     for q in range(8):
         self_ref[q] = own[q * LANES : (q + 1) * LANES, 0:width].T
 
@@ -254,30 +272,36 @@
     return pl.pallas_call(
         functools.partial(gather_kernel, nb),
         out_shape=(
-            jax.ShapeDtypeStruct((nb, 8 * width, LANES), BF16),
+            jax.ShapeDtypeStruct((nb, 8 * width, LANES), F32),
+            jax.ShapeDtypeStruct((nb * 8, LANES), jnp.int32),
             jax.ShapeDtypeStruct((8, width, LANES), F32),
             jax.ShapeDtypeStruct((1, 8 * LANES), F32),
             jax.ShapeDtypeStruct((2 * width, wn.shape[1]), BF16),
             jax.ShapeDtypeStruct((8, CLASSES + 16), F32),
         ),
-        in_specs=[vmem, pl.BlockSpec(memory_space=pl.ANY)] + [vmem] * 6,
-        out_specs=(vmem,) * 5,
+        in_specs=[pl.BlockSpec(memory_space=pltpu.HBM)] * 8,
+        out_specs=(vmem,) * 6,
         scratch_shapes=[
             pltpu.VMEM((verts + 8, LANES), F32),
             pltpu.VMEM((nb * 8 * LANES + 8, LANES), F32),
+            pltpu.VMEM(feats.shape, BF16),
+            pltpu.VMEM(ids.shape, jnp.int32),
+            pltpu.VMEM(nbr.shape, jnp.int32),
+            pltpu.VMEM(wn.shape, BF16),
+            pltpu.VMEM(ws.shape, BF16),
+            pltpu.VMEM(dl.shape, F32),
+            pltpu.VMEM(second.shape, jnp.int32),
             pltpu.VMEM((8 * LANES, LANES), F32),
             pltpu.VMEM((total + 64, LANES), jnp.int32),
             pltpu.VMEM((total + 64, LANES), jnp.int32),
-            pltpu.VMEM((nb * 8, LANES), jnp.int32),
             pltpu.VMEM((2, CHUNK + 8, LANES), jnp.int32),
-            pltpu.SMEM((nb * 8, LANES), jnp.int32),
             pltpu.SMEM((2 * (CHUNK + 8), LANES), jnp.int32),
             pltpu.SMEM(front.shape, jnp.int32),
             pltpu.SemaphoreType.DMA((2,)),
             pltpu.SemaphoreType.DMA,
-            pltpu.SemaphoreType.DMA,
+            pltpu.SemaphoreType.DMA((7,)),
         ],
-        compiler_params=pltpu.CompilerParams(vmem_limit_bytes=40 * 1024 * 1024),
+        compiler_params=pltpu.CompilerParams(vmem_limit_bytes=VMEM_BYTES),
         cost_estimate=pl.CostEstimate(flops=200000000, bytes_accessed=100000000, transcendentals=0),
         name="neighbour_sums",
     )(feats, front, ids, nbr, wn, ws, dl, second)
@@ -298,27 +322,33 @@
 
 def layers_kernel(
     nz, ny,
-    part_ref, self_ref, deg_ref, w_ref, side_ref, b1_ref, w2s_ref, w2n_ref, b2_ref,
-    logits_ref, gs_ref, gn_ref,
-    grads_ref, gotw, sv, sall, got1, xs, got2, pre, got3, lp, got4, l2, got5,
-    gp, gotg, gz, gotz, gall, gy,
+    feats_hbm, rest_hbm, pairs_hbm, self_hbm, deg_hbm, w_hbm, side_hbm,
+    b1_hbm, w2s_hbm, w2n_hbm, b2_hbm,
+    out_ref,
+    feats_ref, table, rest, self_ref, deg_ref, w_ref, side_ref,
+    b1_ref, w2s_ref, w2n_ref, b2_ref, load_sems, pairs_s, sums, part_ref, grads_ref, gotw, sv, sall, got1, xs, got2, pre, got3, lp, got4, l2, got5,
+    gp, gotg, gx, gotx, gz, gy,
     sw, rw, sf, rf, sa, ra, sb, rb, s0, r0, s1, r1, s2, r2, s3, r3, s4, r4, s5, r5,
-    sg, rg, sz, rz, sq, rq, sy, ry, sx, rx, sh, rh,
+    sg, rg, sz, rz, sy, ry, sx, rx, sh, rh,
 ):
     feat = lax.axis_index("feat")
     graph = lax.axis_index("graph")
-    ng = part_ref.shape[0]
+    ng = pairs_hbm.shape[0] // 8
     z = feat // ny
     y = feat % ny
     core = graph % 2
-    width = part_ref.shape[1] // 8
+    width = self_ref.shape[1]
     cdim = w2s_ref.shape[0]
     rows = 2 * CLASSES // ng
-    bit = rows // nz
+    nx = ng // 2
+    xat = graph // 2
 
     def at_graph(d):
         return (feat, (graph + d) % ng)
 
+    def at_x(d):
+        return (feat, (graph + 2 * d) % ng)
+
     def at_z(d):
         return (((z + d) % nz) * ny + y, graph)
 
@@ -326,6 +356,15 @@
         return (z * ny + (y + d) % ny, graph)
 
     sibling = (feat, graph + 1 - 2 * core)
+
+    moved = [
+        (feats_hbm, feats_ref), (w_hbm, w_ref), (side_hbm, side_ref), (self_hbm, self_ref),
+        (pairs_hbm, pairs_s), (rest_hbm, rest), (deg_hbm, deg_ref), (b1_hbm, b1_ref),
+        (w2s_hbm, w2s_ref), (w2n_hbm, w2n_ref), (b2_hbm, b2_ref),
+    ]
+    loads = [pltpu.make_async_copy(a, b, load_sems.at[i]) for i, (a, b) in enumerate(moved)]
+    for load in loads:
+        load.start()
 
     barrier = pltpu.get_barrier_semaphore()
     for d in range(1, ng):
@@ -334,6 +373,34 @@
         pl.semaphore_signal(barrier, inc=1, device_id=at_z(d), device_id_type=MESH)
     for d in range(1, ny):
         pl.semaphore_signal(barrier, inc=1, device_id=at_y(d), device_id_type=MESH)
+
+    targets = 8 * LANES
+
+    def batch_sums(d):
+        b = (graph + d) % ng
+
+        def tile(q, c):
+            r = b * 8 + q
+            into = pl.multiple_of(q * LANES, LANES)
+            for at in range(0, LANES, DENSE):
+                words = [pairs_s[r, at + u] for u in range(DENSE)]
+                got = [
+                    table[pl.ds(w & (WORD - 1), 1), :]
+                    + table[pl.ds(w >> WORD_BITS, 1), :]
+                    for w in words
+                ]
+                for u in range(DENSE):
+                    sums[pl.ds(into + at + u, 1), :] = got[u]
+            return c
+
+        lax.fori_loop(0, 8, tile, 0)
+        turned = [sums[q * LANES : (q + 1) * LANES, 0:width].T for q in range(8)]
+        part_ref[b] = (jnp.concatenate(turned, axis=0) + rest[b]).astype(BF16)
+
+    loads[0].wait()
+    build_table(feats_ref, table)
+    for load in loads[1:4]:
+        load.wait()
     pl.semaphore_wait(barrier, (ng - 1) + (nz - 1) + (ny - 1))
 
     def remote(src, dst, ssem, rsem, where):
@@ -347,23 +414,30 @@
         copy.start()
         return copy
 
-    c1 = [
-        send(part_ref.at[(graph + d) % ng], got1.at[d], s1.at[d], r1.at[d], at_graph(d))
-        for d in range(1, ng)
-    ]
-    ca = [send(side_ref, sv.at[z], sa.at[d], ra.at[d], at_z(d)) for d in range(1, nz)]
-
-    def weight_copy(d):
-        return remote(w_ref, gotw.at[z], sw.at[d], rw.at[d], at_z(d))
-
-    def weight_pass(d):
-        block = gotw.at[(z - d + nz) % nz]
-        return remote(block, block, sf.at[d], rf.at[d], sibling)
-
-    @pl.when(z % 2 == core)
-    def _():
-        for d in range(1, nz):
-            weight_copy(d).start()
+    far = nz // 2
+
+    def weight_copy(k):
+        to = ((z + (1 - 2 * core) * k + nz) % nz) * ny + y
+        return remote(w_ref, gotw.at[z], sw.at[k], rw.at[k], (to, graph))
+
+    def weight_pass(k):
+        block = gotw.at[(z - (1 - 2 * core) * k + nz) % nz]
+        return remote(block, block, sf.at[k], rf.at[k], sibling)
+
+    def weight_step(k):
+        def step():
+            weight_copy(k).wait_recv()
+            weight_pass(k).start()
+
+        if k < far:
+            step()
+        else:
+            pl.when(core == 0)(step)
+
+    for k in range(1, far):
+        weight_copy(k).start()
+    pl.when(core == 0)(lambda: weight_copy(far).start())
+    gotw[z] = w_ref[...]
 
     c0 = [
         send(
@@ -372,14 +446,20 @@
         )
         for d in range(1, nz)
     ]
-    gotw[z] = w_ref[...]
     sv[z] = side_ref[...]
     got2[z, width : 2 * width, :] = self_ref[z]
 
-    for c in ca:
-        c.wait_recv()
-    cb = [send(sv, sall.at[y], sb.at[d], rb.at[d], at_y(d)) for d in range(1, ny)]
-    sall[y] = sv[...]
+    ca = [send(side_ref, sv.at[z], sa.at[d], ra.at[d], at_z(d)) for d in range(1, nz)]
+
+    for load in loads[4:]:
+        load.wait()
+    batch_sums(1)
+    c1 = []
+    for d in range(1, ng):
+        c1.append(
+            send(part_ref.at[(graph + d) % ng], got1.at[d], s1.at[d], r1.at[d], at_graph(d))
+        )
+        batch_sums((d + 1) % ng)
 
     summed = part_ref[graph].astype(F32)
     for d in range(1, ng):
@@ -394,12 +474,30 @@
         for d in range(1, nz)
     ]
     got2[z, 0:width, :] = xs[z]
-
-    for d in range(1, nz):
-        @pl.when((z + d) % 2 == core)
-        def _():
-            weight_copy(d).wait_recv()
-            weight_pass(d).start()
+    for c in ca:
+        c.wait_recv()
+    cb = [send(sv, sall.at[y], sb.at[d], rb.at[d], at_y(d)) for d in range(1, ny)]
+    sall[y] = sv[...]
+    for k in range(1, far + 1):
+        weight_step(k)
+
+    for c in c0 + c2:
+        c.wait_recv()
+    x = got2[...].reshape(nz * 2 * width, LANES)
+    for k in range(1, far):
+        weight_pass(k).wait_recv()
+    pl.when(core == 1)(lambda: weight_pass(far).wait_recv())
+    w = gotw[...].reshape(nz * 2 * width, w_ref.shape[1])
+    high = x.astype(BF16)
+    low = (x - high.astype(F32)).astype(BF16)
+    part = lax.dot_general(high, w, TN, preferred_element_type=F32) + lax.dot_general(
+        low, w, TN, preferred_element_type=F32
+    )
+    for k in range(ny):
+        pre[k] = part[:, k * LANES : (k + 1) * LANES]
+    c3 = [
+        send(pre.at[(y + d) % ny], got3.at[d], s3.at[d], r3.at[d], at_y(d)) for d in range(1, ny)
+    ]
 
     for c in cb:
         c.wait_recv()
@@ -418,25 +516,6 @@
     row = ((at // 8) % nz) * (ny * 8) + (at // (8 * nz)) * 8 + at % 8
     same = jnp.where(row == spot, 1.0, 0.0).astype(BF16)
 
-    for c in c0 + c2:
-        c.wait_recv()
-    x = got2[...].reshape(nz * 2 * width, LANES)
-    for d in range(1, nz):
-        @pl.when((z + d) % 2 != core)
-        def _():
-            weight_pass(d).wait_recv()
-    w = gotw[...].reshape(nz * 2 * width, w_ref.shape[1])
-    high = x.astype(BF16)
-    low = (x - high.astype(F32)).astype(BF16)
-    part = lax.dot_general(high, w, TN, preferred_element_type=F32) + lax.dot_general(
-        low, w, TN, preferred_element_type=F32
-    )
-    for k in range(ny):
-        pre[k] = part[:, k * LANES : (k + 1) * LANES]
-    c3 = [
-        send(pre.at[(y + d) % ny], got3.at[d], s3.at[d], r3.at[d], at_y(d)) for d in range(1, ny)
-    ]
-
     def exact(wide, ones):
         total = jnp.zeros((wide.shape[1], ones.shape[1]), F32)
         for _ in range(3):
@@ -458,23 +537,23 @@
     g = jnp.dot(cot_high, h, preferred_element_type=F32) + jnp.dot(
         cot_low, h, preferred_element_type=F32
     )
-    gp[...] = g.reshape(ng, rows, LANES)
-    cg = [
-        send(gp.at[(graph + d) % ng], gotg.at[d], sg.at[d], rg.at[d], at_graph(d))
-        for d in range(1, ng)
-    ]
+    gp[...] = g.reshape(nx, 2, rows, LANES)
+    cg = [send(gp.at[:, 1 - core], gotg, sg.at[0], rg.at[0], sibling)]
+    cg[0].wait_recv()
+    gx[...] = gp[:, core] + gotg[...]
+    for d in range(1, nx):
+        cg.append(send(gx.at[(xat + d) % nx], gotx.at[d], sg.at[d], rg.at[d], at_x(d)))
 
     columns = pl.ds(pl.multiple_of(y * LANES, LANES), LANES)
     zs = lax.dot_general(h, w2s_ref[:, columns], NT, preferred_element_type=F32)
     zn = lax.dot_general(h, w2n_ref[:, columns], NT, preferred_element_type=F32)
 
-    gsum = gp[graph]
-    for d in range(1, ng):
-        cg[d - 1].wait_recv()
-        gsum = gsum + gotg[d]
-    for k in range(nz):
-        gz[k] = gsum[k * bit : (k + 1) * bit]
-    cz = [send(gz.at[(z + d) % nz], gotz.at[d], sz.at[d], rz.at[d], at_z(d)) for d in range(1, nz)]
+    gsum = gx[xat]
+    for d in range(1, nx):
+        cg[d].wait_recv()
+        gsum = gsum + gotx[d]
+    gz[z] = gsum
+    cz = [send(gz.at[z], gz.at[z], sz.at[d], rz.at[d], at_z(d)) for d in range(1, nz)]
 
     scores = split_dot(hits, zn, NN) / deg2 + split_dot(same, zs, NN)
     lp[...] = scores.reshape(ny, nz, 8, cdim)
@@ -482,12 +561,13 @@
         send(lp.at[(y + d) % ny], got4.at[d], s4.at[d], r4.at[d], at_y(d)) for d in range(1, ny)
     ]
 
-    whole = gz[z]
-    for d in range(1, nz):
-        cz[d - 1].wait_recv()
-        whole = whole + gotz[d]
-    gall[z] = whole
-    cq = [send(gall.at[z], gall.at[z], sq.at[d], rq.at[d], at_z(d)) for d in range(1, nz)]
+    for c in cz:
+        c.wait_recv()
+    whole = gz[0]
+    for k in range(1, nz):
+        whole = whole + gz[k]
+    gy[y] = whole
+    cy = [send(gy.at[y], gy.at[y], sy.at[d], ry.at[d], at_y(d)) for d in range(1, ny)]
 
     lsum = lp[y]
     for d in range(1, ny):
@@ -498,56 +578,46 @@
         send(l2.at[(z + d) % nz], got5.at[d], s5.at[d], r5.at[d], at_z(d)) for d in range(1, nz)
     ]
 
-    for c in cq:
-        c.wait_recv()
-    gy[y] = jnp.concatenate([gall[k] for k in range(nz)], axis=0)
-    cy = [send(gy.at[y], gy.at[y], sy.at[d], ry.at[d], at_y(d)) for d in range(1, ny)]
     for c in cy:
         c.wait_recv()
-    grads_ref[graph] = gy[...].reshape(ny * rows, LANES).astype(BF16)
-    mine = grads_ref.at[graph]
-    cx = [send(mine, mine, sx.at[d], rx.at[d], at_graph(2 * d)) for d in range(1, ng // 2)]
-    ch = [send(mine, mine, sh.at[0], rh.at[0], sibling)]
+    grads_ref[core, xat] = gy[...].reshape(ny * rows, LANES).astype(BF16)
+    mine = grads_ref.at[core, xat]
+    cx = [send(mine, mine, sx.at[d], rx.at[d], at_x(d)) for d in range(1, nx)]
 
     final = l2[z] + b2_ref[...]
     for d in range(1, nz):
         c5[d - 1].wait_recv()
         final = final + got5[d]
-    logits_ref[...] = final
-
-    for d in range(1, ng // 2):
-        cx[d - 1].wait_recv()
-        block = grads_ref.at[(graph + ng - 2 * d) % ng]
-        ch.append(send(block, block, sh.at[d], rh.at[d], sibling))
-    for c in ch:
+    out_ref[2 * CLASSES : 2 * CLASSES + 8, 0:cdim] = final
+
+    for c in cx:
         c.wait_recv()
-    half = ng // 2
+    mine = grads_ref.at[core]
+    ch = [send(mine, mine, sh.at[0], rh.at[0], sibling)]
+    ch[0].wait_recv()
     for k in range(ng):
-        out = gs_ref if k < half else gn_ref
-        base = (k % half) * rows
-        keep = min(rows, cdim - base)
-        block = grads_ref[k].astype(F32)
+        block = grads_ref[k % 2, k // 2].astype(F32)
         for j in range(ny):
-            out[base : base + keep, j * LANES : (j + 1) * LANES] = block[
-                j * rows : j * rows + keep
+            out_ref[k * rows : (k + 1) * rows, j * LANES : (j + 1) * LANES] = block[
+                j * rows : (j + 1) * rows
             ]
-    for c in ca + cb + c0 + c1 + c2 + c3 + cg + c4 + cz + cq + c5 + cy + cx + ch:
+    for c in ca + cb + c0 + c1 + c2 + c3 + cg + c4 + cz + c5 + cy + cx + ch:
         c.wait_send()
 
-    @pl.when(z % 2 == core)
+    for k in range(1, far):
+        weight_copy(k).wait_send()
+        weight_pass(k).wait_send()
+
+    @pl.when(core == 0)
     def _():
-        for d in range(1, nz):
-            weight_copy(d).wait_send()
-
-    for d in range(1, nz):
-        @pl.when((z + d) % 2 == core)
-        def _():
-            weight_pass(d).wait_send()
-
-
-def layers(nz, ny, part, own, deg, w, side, b1, w2s, w2n, b2):
-    ng, rows, _ = part.shape
-    width = rows // 8
+        weight_copy(far).wait_send()
+        weight_pass(far).wait_send()
+
+
+def layers(nz, ny, feats, rest, pairs, own, deg, w, side, b1, w2s, w2n, b2):
+    ng = pairs.shape[0] // 8
+    width = own.shape[1]
+    rows = 8 * width
     cdim = w2s.shape[0]
     cut = 2 * CLASSES // ng
     vmem = pl.BlockSpec(memory_space=pltpu.VMEM)
@@ -555,15 +625,26 @@
     pair = lambda n: [dma(n), dma(n)]
     return pl.pallas_call(
         functools.partial(layers_kernel, nz, ny),
-        out_shape=(
-            jax.ShapeDtypeStruct((8, cdim), F32),
-            jax.ShapeDtypeStruct(w2s.shape, F32),
-            jax.ShapeDtypeStruct(w2n.shape, F32),
-        ),
-        in_specs=[vmem] * 9,
-        out_specs=(vmem, vmem, vmem),
+        out_shape=jax.ShapeDtypeStruct((2 * CLASSES + 8, w2s.shape[1]), F32),
+        in_specs=[pl.BlockSpec(memory_space=pltpu.HBM)] * 11,
+        out_specs=vmem,
         scratch_shapes=[
-            pltpu.VMEM((ng, ny * cut, LANES), BF16),
+            pltpu.VMEM(feats.shape, BF16),
+            pltpu.VMEM((feats.shape[1] + 8, LANES), F32),
+            pltpu.VMEM(rest.shape, F32),
+            pltpu.VMEM(own.shape, F32),
+            pltpu.VMEM(deg.shape, F32),
+            pltpu.VMEM(w.shape, BF16),
+            pltpu.VMEM(side.shape, F32),
+            pltpu.VMEM(b1.shape, F32),
+            pltpu.VMEM(w2s.shape, BF16),
+            pltpu.VMEM(w2n.shape, BF16),
+            pltpu.VMEM(b2.shape, F32),
+            pltpu.SemaphoreType.DMA((11,)),
+            pltpu.SMEM(pairs.shape, jnp.int32),
+            pltpu.VMEM((8 * LANES, LANES), F32),
+            pltpu.VMEM((ng, rows, LANES), BF16),
+            pltpu.VMEM((2, ng // 2, ny * cut, LANES), BF16),
             pltpu.VMEM((nz, 2 * width, w.shape[1]), BF16),
             pltpu.VMEM((nz,) + side.shape, F32),
             pltpu.VMEM((ny, nz) + side.shape, F32),
@@ -576,22 +657,21 @@
             pltpu.VMEM((ny, nz, 8, cdim), F32),
             pltpu.VMEM((nz, 8, cdim), F32),
             pltpu.VMEM((nz, 8, cdim), F32),
-            pltpu.VMEM((ng, cut, LANES), F32),
-            pltpu.VMEM((ng, cut, LANES), F32),
-            pltpu.VMEM((nz, cut // nz, LANES), F32),
-            pltpu.VMEM((nz, cut // nz, LANES), F32),
-            pltpu.VMEM((nz, cut // nz, LANES), F32),
+            pltpu.VMEM((ng // 2, 2, cut, LANES), F32),
+            pltpu.VMEM((ng // 2, cut, LANES), F32),
+            pltpu.VMEM((ng // 2, cut, LANES), F32),
+            pltpu.VMEM((ng // 2, cut, LANES), F32),
+            pltpu.VMEM((nz, cut, LANES), F32),
             pltpu.VMEM((ny, cut, LANES), F32),
         ]
         + pair(nz) + pair(nz) + pair(nz) + pair(ny) + pair(nz) + pair(ng) + pair(nz)
-        + pair(ny) + pair(ny) + pair(nz) + pair(ng) + pair(nz) + pair(nz) + pair(ny)
-        + pair(ng) + pair(ng),
+        + pair(ny) + pair(ny) + pair(nz) + pair(ng) + pair(nz) + pair(ny) + pair(ng) + pair(1),
         compiler_params=pltpu.CompilerParams(
-            collective_id=0, has_side_effects=True, vmem_limit_bytes=40 * 1024 * 1024
+            collective_id=0, has_side_effects=True, vmem_limit_bytes=VMEM_BYTES
         ),
         cost_estimate=pl.CostEstimate(flops=300000000, bytes_accessed=10000000, transcendentals=0),
         name="layers",
-    )(part, own, deg, w, side, b1, w2s, w2n, b2)
+    )(feats, rest, pairs, own, deg, w, side, b1, w2s, w2n, b2)
 
 
 def on_device(feats, front_ids, nbr1, nbr2, w1_self, w1_neigh, b1, w2_self, w2_neigh, b2, dlogits):
@@ -600,16 +680,20 @@
     hidden, cdim = w2_self.shape
     nz, ny = 8, 4
 
-    part, own, deg, w, side = gather(
-        feats, front_ids.reshape(-1), front_ids[:, 0, :], nbr1.transpose(2, 0, 1),
+    rest, pairs, own, deg, w, side = gather(
+        feats, front_ids.reshape(-1), front_ids, nbr1.transpose(2, 0, 1),
         w1_neigh, w1_self,
         dlogits[0], nbr2[0], nb,
     )
-    logits, grad_s, grad_n = layers(
-        nz, ny, part, own, deg, w, side,
+    out = layers(
+        nz, ny, feats, rest, pairs, own, deg, w, side,
         b1.reshape(ny, 1, LANES), w2_self.T, w2_neigh.T, b2.reshape(1, cdim),
     )
-    return (logits[None], grad_s.T, grad_n.T)
+    return (
+        out[None, 2 * CLASSES :, :cdim],
+        out[:cdim].T,
+        out[CLASSES : CLASSES + cdim].T,
+    )
 
 
 def solution(mesh):

time: 94.8 us -> 84.8 us (0.89)
  Pallas kernels: 87.7 us -> 80.8 us
  local copies, waits for them, and re-layouts: 6.07 us -> 3.24 us
    pallas_call x1, Pallas kernels: 33.7 us -> 21.5 us  [gather(): pl.pallas_call(functools.partial(gather_kernel, nb), out_shape=(jax.Shape...]
    unnamed x26 -> x0, local copies, waits for them, and re-layouts: 6.07 us -> none
    pallas_call x1, Pallas kernels: 54 us -> 59.3 us  [layers(): pl.pallas_call(functools.partial(layers_kernel, nz, ny), out_shape=jax.Sh...]
    transpose x0 -> x1, local copies, waits for them, and re-layouts: none -> 1.95 us  [on_device(): out[CLASSES:CLASSES + cdim]]
    broadcast_in_dim x0 -> x1, local copies, waits for them, and re-layouts: none -> 1.3 us  [on_device(): out[None, 2 * CLASSES:, :cdim]]
where the time goes in v4:
time: 84.8 us; the launch traced here: 84.6 us
  Pallas kernels  80.8 us (95%)
  local copies, waits for them, and re-layouts  3.24 us (4%)
    pallas_call x1, Pallas kernels, layers(): pl.pallas_call(functools.partial(layers_kernel, nz, ny), out_shape=jax.Sh...  59.3 us
    pallas_call x1, Pallas kernels, gather(): pl.pallas_call(functools.partial(gather_kernel, nb), out_shape=(jax.Shape...  21.5 us
    transpose x1, local copies, waits for them, and re-layouts, on_device(): out[CLASSES:CLASSES + cdim]  1.95 us

profile of v4, /device:TPU:1, one launch (start us, length us, event | category | flops | bytes accessed | tf_op | source)
XLA Modules:
  0.0 84.6 jit_solution(13379347120231333947)
XLA Ops:
  0.6 21.5 %neighbour_sums.1 = (f32[8,192,128]{2,1,0:T(8,128)}, s32[64,128]{1,0:T(8,128)}, f32[8,24,128]{2,1,0:T(8,128)}, f32[1,1024]{1,0:T(1,128)}, bf16[48,512]{1,0:T(8,128)(2,1)}, /*index=5*/f32[8,176]{1,0:T(8,128)}) custom-call(bf16[24,16384]{1,0:T(8,128)(2,1)} %feats_hbm.3, s32[32768]{0:T(1024)} %bitcast.15, s32[8,1,4096]{2,1,0:T(1,128)} %ids_hbm.1, ...), custom_call_target="tpu_custom_call" | custom-call | flops 200000000 | bytes 100000000 | tf_op jit(solution)/shard_map/neighbour_sums/pallas_call | solution.py:272
  22.1 59.3 %layers.1 = f32[328,512]{1,0:T(8,128)} custom-call(bf16[24,16384]{1,0:T(8,128)(2,1)} %feats_hbm.3, f32[8,192,128]{2,1,0:T(8,128)} %get-tuple-element.9.rest_hbm, s32[64,128]{1,0:T(8,128)} %get-tuple-element.10.pairs_hbm, f32[8,24,128]{2,1,0:T(8,128)} %get-tuple-element.11.self_hbm, f32[1,1024]{1,0:T(1,128)} %get-tuple-element.12.deg_hbm, ...), custom_call_target="tpu_custom_call" | custom-call | flops 300000000 | bytes 10000000 | tf_op jit(solution)/shard_map/layers/pallas_call | solution.py:626
  81.4 1.3 %slice_bitcast_fusion.2 = f32[1,8,153]{2,1,0:T(8,128)} fusion(f32[328,512]{1,0:T(8,128)} %layers.1), kind=kLoop, calls=%fused_computation.2 | loop fusion | bytes 9792 | tf_op jit(solution)/shard_map/broadcast_in_dim | solution.py:693
  82.7 1.9 %slice_bitcast_fusion = (f32[512,153]{0,1:T(8,128)}, f32[512,153]{0,1:T(8,128)}) fusion(f32[328,512]{1,0:T(8,128)} %layers.1), kind=kLoop, calls=%fused_computation | loop fusion | bytes 1253376 | tf_op jit(solution)/shard_map/transpose | solution.py:695

commit v5 on v4

--- a/solution.py
+++ b/solution.py
@@ -15,6 +15,7 @@
 VMEM_BYTES = 60 * 1024 * 1024
 FAN2 = 15
 DENSE = 8
+OWN = 16
 WORD_BITS = 15
 WORD = 1 << WORD_BITS
 MESH = pl.DeviceIdType.MESH
@@ -42,8 +43,8 @@
 
 def gather_kernel(
     nb, feats_hbm, front_ref, ids_hbm, nbr_hbm, wn_hbm, ws_hbm, dl_hbm, second_hbm,
-    rest_ref, pairs_v, self_ref, deg_ref, w_ref, side_ref,
-    table, acc, feats_ref, ids_ref, nbr_ref, wn_ref, ws_ref, dl_ref, second_ref, own, one, two, lists_v, lists_s, front_s,
+    rest_ref, pairs_v, deg_ref, w_ref, side_ref,
+    table, acc, feats_ref, ids_ref, nbr_ref, wn_ref, ws_ref, dl_ref, second_ref, one, two, lists_v, lists_s, front_s,
     sems, front_sem, load_sems,
 ):
     width = feats_ref.shape[0]
@@ -246,23 +247,12 @@
 
     lax.fori_loop(0, chunks, chunk, 0)
 
-    def mine(i, c):
-        base = graph * fs + i * UNROLL
-        got = [table[pl.ds(front_s[base + u], 1), :] for u in range(UNROLL)]
-        for u in range(UNROLL):
-            own[pl.ds(i * UNROLL + u, 1), :] = got[u]
-        return c
-
-    lax.fori_loop(0, targets // UNROLL, mine, 0)
-
     for b in range(nb):
         turned = [
             acc[b * targets + q * LANES : b * targets + (q + 1) * LANES, 0:width].T
             for q in range(8)
         ]
         rest_ref[b] = jnp.concatenate(turned, axis=0)
-    for q in range(8):
-        self_ref[q] = own[q * LANES : (q + 1) * LANES, 0:width].T
 
 
 def gather(feats, front, ids, nbr, wn, ws, dl, second, nb):
@@ -274,13 +264,12 @@
         out_shape=(
             jax.ShapeDtypeStruct((nb, 8 * width, LANES), F32),
             jax.ShapeDtypeStruct((nb * 8, LANES), jnp.int32),
-            jax.ShapeDtypeStruct((8, width, LANES), F32),
             jax.ShapeDtypeStruct((1, 8 * LANES), F32),
             jax.ShapeDtypeStruct((2 * width, wn.shape[1]), BF16),
             jax.ShapeDtypeStruct((8, CLASSES + 16), F32),
         ),
         in_specs=[pl.BlockSpec(memory_space=pltpu.HBM)] * 8,
-        out_specs=(vmem,) * 6,
+        out_specs=(vmem,) * 5,
         scratch_shapes=[
             pltpu.VMEM((verts + 8, LANES), F32),
             pltpu.VMEM((nb * 8 * LANES + 8, LANES), F32),
@@ -291,7 +280,6 @@
             pltpu.VMEM(ws.shape, BF16),
             pltpu.VMEM(dl.shape, F32),
             pltpu.VMEM(second.shape, jnp.int32),
-            pltpu.VMEM((8 * LANES, LANES), F32),
             pltpu.VMEM((total + 64, LANES), jnp.int32),
             pltpu.VMEM((total + 64, LANES), jnp.int32),
             pltpu.VMEM((2, CHUNK + 8, LANES), jnp.int32),
@@ -322,14 +310,14 @@
 
 def layers_kernel(
     nz, ny,
-    feats_hbm, rest_hbm, pairs_hbm, self_hbm, deg_hbm, w_hbm, side_hbm,
+    feats_hbm, front_hbm, rest_hbm, pairs_hbm, deg_hbm, w_hbm, side_hbm,
     b1_hbm, w2s_hbm, w2n_hbm, b2_hbm,
     out_ref,
     feats_ref, table, rest, self_ref, deg_ref, w_ref, side_ref,
-    b1_ref, w2s_ref, w2n_ref, b2_ref, load_sems, pairs_s, sums, part_ref, grads_ref, gotw, sv, sall, got1, xs, got2, pre, got3, lp, got4, l2, got5,
+    b1_ref, w2s_ref, w2n_ref, b2_ref, load_sems, pairs_s, own_s, sums, part_ref, grads_ref, gotw, sv, sall, got1, xs, got2, pre, got3, lp, got4, l2, got5,
     gp, gotg, gx, gotx, gz, gy,
     sw, rw, sf, rf, sa, ra, sb, rb, s0, r0, s1, r1, s2, r2, s3, r3, s4, r4, s5, r5,
-    sg, rg, sz, rz, sy, ry, sx, rx, sh, rh,
+    sg, rg, sz, rz, sy, ry, sx, rx,
 ):
     feat = lax.axis_index("feat")
     graph = lax.axis_index("graph")
@@ -337,7 +325,8 @@
     z = feat // ny
     y = feat % ny
     core = graph % 2
-    width = self_ref.shape[1]
+    width = feats_hbm.shape[0]
+    fs = front_hbm.shape[0] // ng
     cdim = w2s_ref.shape[0]
     rows = 2 * CLASSES // ng
     nx = ng // 2
@@ -358,8 +347,8 @@
     sibling = (feat, graph + 1 - 2 * core)
 
     moved = [
-        (feats_hbm, feats_ref), (w_hbm, w_ref), (side_hbm, side_ref), (self_hbm, self_ref),
-        (pairs_hbm, pairs_s), (rest_hbm, rest), (deg_hbm, deg_ref), (b1_hbm, b1_ref),
+        (feats_hbm, feats_ref), (w_hbm, w_ref), (side_hbm, side_ref),
+        (front_hbm.at[pl.ds(pl.multiple_of(graph * fs, fs), 8 * LANES)], own_s), (pairs_hbm, pairs_s), (rest_hbm, rest), (deg_hbm, deg_ref), (b1_hbm, b1_ref),
         (w2s_hbm, w2s_ref), (w2n_hbm, w2n_ref), (b2_hbm, b2_ref),
     ]
     loads = [pltpu.make_async_copy(a, b, load_sems.at[i]) for i, (a, b) in enumerate(moved)]
@@ -399,7 +388,7 @@
 
     loads[0].wait()
     build_table(feats_ref, table)
-    for load in loads[1:4]:
+    for load in loads[1:3]:
         load.wait()
     pl.semaphore_wait(barrier, (ng - 1) + (nz - 1) + (ny - 1))
 
@@ -439,19 +428,11 @@
     pl.when(core == 0)(lambda: weight_copy(far).start())
     gotw[z] = w_ref[...]
 
-    c0 = [
-        send(
-            self_ref.at[(z + d) % nz], got2.at[z, pl.ds(width, width)],
-            s0.at[d], r0.at[d], at_z(d),
-        )
-        for d in range(1, nz)
-    ]
     sv[z] = side_ref[...]
-    got2[z, width : 2 * width, :] = self_ref[z]
 
     ca = [send(side_ref, sv.at[z], sa.at[d], ra.at[d], at_z(d)) for d in range(1, nz)]
 
-    for load in loads[4:]:
+    for load in loads[3:]:
         load.wait()
     batch_sums(1)
     c1 = []
@@ -460,6 +441,24 @@
             send(part_ref.at[(graph + d) % ng], got1.at[d], s1.at[d], r1.at[d], at_graph(d))
         )
         batch_sums((d + 1) % ng)
+
+    def mine(i, c):
+        got = [table[pl.ds(own_s[i * OWN + u], 1), :] for u in range(OWN)]
+        for u in range(OWN):
+            sums[pl.ds(pl.multiple_of(i * OWN, OWN) + u, 1), :] = got[u]
+        return c
+
+    lax.fori_loop(0, targets // OWN, mine, 0)
+    for q in range(8):
+        self_ref[q] = sums[q * LANES : (q + 1) * LANES, 0:width].T
+    c0 = [
+        send(
+            self_ref.at[(z + d) % nz], got2.at[z, pl.ds(width, width)],
+            s0.at[d], r0.at[d], at_z(d),
+        )
+        for d in range(1, nz)
+    ]
+    got2[z, width : 2 * width, :] = self_ref[z]
 
     summed = part_ref[graph].astype(F32)
     for d in range(1, ng):
@@ -580,28 +579,29 @@
 
     for c in cy:
         c.wait_recv()
-    grads_ref[core, xat] = gy[...].reshape(ny * rows, LANES).astype(BF16)
-    mine = grads_ref.at[core, xat]
-    cx = [send(mine, mine, sx.at[d], rx.at[d], at_x(d)) for d in range(1, nx)]
-
+    grads_ref[graph] = gy[...].reshape(ny * rows, LANES).astype(BF16)
+    mine = grads_ref.at[graph]
+    cx = [send(mine, mine, sx.at[d], rx.at[d], at_graph(d)) for d in range(1, ng)]
+
+    def emit(k):
+        block = grads_ref[k].astype(F32)
+        base = pl.multiple_of(k * rows, 8)
+        for j in range(ny):
+            out_ref[pl.ds(base, rows), j * LANES : (j + 1) * LANES] = block[
+                j * rows : (j + 1) * rows
+            ]
+
+    emit(graph)
     final = l2[z] + b2_ref[...]
     for d in range(1, nz):
         c5[d - 1].wait_recv()
         final = final + got5[d]
     out_ref[2 * CLASSES : 2 * CLASSES + 8, 0:cdim] = final
 
-    for c in cx:
-        c.wait_recv()
-    mine = grads_ref.at[core]
-    ch = [send(mine, mine, sh.at[0], rh.at[0], sibling)]
-    ch[0].wait_recv()
-    for k in range(ng):
-        block = grads_ref[k % 2, k // 2].astype(F32)
-        for j in range(ny):
-            out_ref[k * rows : (k + 1) * rows, j * LANES : (j + 1) * LANES] = block[
-                j * rows : (j + 1) * rows
-            ]
-    for c in ca + cb + c0 + c1 + c2 + c3 + cg + c4 + cz + c5 + cy + cx + ch:
+    for d in range(1, ng):
+        cx[d - 1].wait_recv()
+        emit((graph - d + ng) % ng)
+    for c in ca + cb + c0 + c1 + c2 + c3 + cg + c4 + cz + c5 + cy + cx:
         c.wait_send()
 
     for k in range(1, far):
@@ -614,9 +614,9 @@
         weight_pass(far).wait_send()
 
 
-def layers(nz, ny, feats, rest, pairs, own, deg, w, side, b1, w2s, w2n, b2):
+def layers(nz, ny, feats, front, rest, pairs, deg, w, side, b1, w2s, w2n, b2):
     ng = pairs.shape[0] // 8
-    width = own.shape[1]
+    width = feats.shape[0]
     rows = 8 * width
     cdim = w2s.shape[0]
     cut = 2 * CLASSES // ng
@@ -632,7 +632,7 @@
             pltpu.VMEM(feats.shape, BF16),
             pltpu.VMEM((feats.shape[1] + 8, LANES), F32),
             pltpu.VMEM(rest.shape, F32),
-            pltpu.VMEM(own.shape, F32),
+            pltpu.VMEM((8, width, LANES), F32),
             pltpu.VMEM(deg.shape, F32),
             pltpu.VMEM(w.shape, BF16),
             pltpu.VMEM(side.shape, F32),
@@ -642,9 +642,10 @@
             pltpu.VMEM(b2.shape, F32),
             pltpu.SemaphoreType.DMA((11,)),
             pltpu.SMEM(pairs.shape, jnp.int32),
+            pltpu.SMEM((8 * LANES,), jnp.int32),
             pltpu.VMEM((8 * LANES, LANES), F32),
             pltpu.VMEM((ng, rows, LANES), BF16),
-            pltpu.VMEM((2, ng // 2, ny * cut, LANES), BF16),
+            pltpu.VMEM((ng, ny * cut, LANES), BF16),
             pltpu.VMEM((nz, 2 * width, w.shape[1]), BF16),
             pltpu.VMEM((nz,) + side.shape, F32),
             pltpu.VMEM((ny, nz) + side.shape, F32),
@@ -665,13 +666,13 @@
             pltpu.VMEM((ny, cut, LANES), F32),
         ]
         + pair(nz) + pair(nz) + pair(nz) + pair(ny) + pair(nz) + pair(ng) + pair(nz)
-        + pair(ny) + pair(ny) + pair(nz) + pair(ng) + pair(nz) + pair(ny) + pair(ng) + pair(1),
+        + pair(ny) + pair(ny) + pair(nz) + pair(ng) + pair(nz) + pair(ny) + pair(ng),
         compiler_params=pltpu.CompilerParams(
             collective_id=0, has_side_effects=True, vmem_limit_bytes=VMEM_BYTES
         ),
         cost_estimate=pl.CostEstimate(flops=300000000, bytes_accessed=10000000, transcendentals=0),
         name="layers",
-    )(feats, rest, pairs, own, deg, w, side, b1, w2s, w2n, b2)
+    )(feats, front, rest, pairs, deg, w, side, b1, w2s, w2n, b2)
 
 
 def on_device(feats, front_ids, nbr1, nbr2, w1_self, w1_neigh, b1, w2_self, w2_neigh, b2, dlogits):
@@ -680,13 +681,14 @@
     hidden, cdim = w2_self.shape
     nz, ny = 8, 4
 
-    rest, pairs, own, deg, w, side = gather(
-        feats, front_ids.reshape(-1), front_ids, nbr1.transpose(2, 0, 1),
+    front = front_ids.reshape(-1)
+    rest, pairs, deg, w, side = gather(
+        feats, front, front_ids, nbr1.transpose(2, 0, 1),
         w1_neigh, w1_self,
         dlogits[0], nbr2[0], nb,
     )
     out = layers(
-        nz, ny, feats, rest, pairs, own, deg, w, side,
+        nz, ny, feats, front, rest, pairs, deg, w, side,
         b1.reshape(ny, 1, LANES), w2_self.T, w2_neigh.T, b2.reshape(1, cdim),
     )
     return (

time: 84.8 us -> 84.6 us (level)
    pallas_call x1, Pallas kernels: 21.5 us -> 19.1 us  [gather(): pl.pallas_call(functools.partial(gather_kernel, nb), out_shape=(jax.Shape...]
    pallas_call x1, Pallas kernels: 59.3 us -> 61.4 us  [layers(): pl.pallas_call(functools.partial(layers_kernel, nz, ny), out_shape=jax.Sh...]
where the time goes in v5:
time: 84.6 us; the launch traced here: 84.4 us
  Pallas kernels  80.5 us (95%)
  local copies, waits for them, and re-layouts  3.24 us (4%)
    pallas_call x1, Pallas kernels, layers(): pl.pallas_call(functools.partial(layers_kernel, nz, ny), out_shape=jax.Sh...  61.4 us
    pallas_call x1, Pallas kernels, gather(): pl.pallas_call(functools.partial(gather_kernel, nb), out_shape=(jax.Shape...  19.1 us
    transpose x1, local copies, waits for them, and re-layouts, on_device(): out[CLASSES:CLASSES + cdim]  1.95 us

profile of v5, /device:TPU:1, one launch (start us, length us, event | category | flops | bytes accessed | tf_op | source)
XLA Modules:
  0.0 84.4 jit_solution(6889695638374226550)
XLA Ops:
  0.6 19.1 %neighbour_sums.1 = (f32[8,192,128]{2,1,0:T(8,128)}, s32[64,128]{1,0:T(8,128)}, f32[1,1024]{1,0:T(1,128)}, bf16[48,512]{1,0:T(8,128)(2,1)}, f32[8,176]{1,0:T(8,128)}) custom-call(bf16[24,16384]{1,0:T(8,128)(2,1)} %feats_hbm.3, s32[32768]{0:T(1024)} %bitcast.14, s32[8,1,4096]{2,1,0:T(1,128)} %ids_hbm.1, s32[25,8,1024]{2,1,0:T(8,128)} %bitcast.16, ...), custom_call_target="tpu_custom_call" | custom-call | flops 200000000 | bytes 100000000 | tf_op jit(solution)/shard_map/neighbour_sums/pallas_call | solution.py:262
  19.8 61.4 %layers.1 = f32[328,512]{1,0:T(8,128)} custom-call(bf16[24,16384]{1,0:T(8,128)(2,1)} %feats_hbm.3, s32[32768]{0:T(1024)} %bitcast.15, f32[8,192,128]{2,1,0:T(8,128)} %get-tuple-element.8.rest_hbm, s32[64,128]{1,0:T(8,128)} %get-tuple-element.9.pairs_hbm, f32[1,1024]{1,0:T(1,128)} %get-tuple-element.10.deg_hbm, bf16[48,512]{1,0:T(8,128)(2,1)} %get-tuple-element.11.w_hbm, ...), custom_call_target="tpu_custom_call" | custom-call | flops 300000000 | bytes 10000000 | tf_op jit(solution)/shard_map/layers/pallas_call | solution.py:626
  81.1 1.3 %slice_bitcast_fusion.2 = f32[1,8,153]{2,1,0:T(8,128)} fusion(f32[328,512]{1,0:T(8,128)} %layers.1), kind=kLoop, calls=%fused_computation.2 | loop fusion | bytes 9792 | tf_op jit(solution)/shard_map/broadcast_in_dim | solution.py:695
  82.4 1.9 %slice_bitcast_fusion = (f32[512,153]{0,1:T(8,128)}, f32[512,153]{0,1:T(8,128)}) fusion(f32[328,512]{1,0:T(8,128)} %layers.1), kind=kLoop, calls=%fused_computation | loop fusion | bytes 1253376 | tf_op jit(solution)/shard_map/transpose | solution.py:697

commit v6 on v5

--- a/solution.py
+++ b/solution.py
@@ -441,6 +441,11 @@
             send(part_ref.at[(graph + d) % ng], got1.at[d], s1.at[d], r1.at[d], at_graph(d))
         )
         batch_sums((d + 1) % ng)
+        if d == ng // 2:
+            for c in ca:
+                c.wait_recv()
+            cb = [send(sv, sall.at[y], sb.at[d], rb.at[d], at_y(d)) for d in range(1, ny)]
+            sall[y] = sv[...]
 
     def mine(i, c):
         got = [table[pl.ds(own_s[i * OWN + u], 1), :] for u in range(OWN)]
@@ -473,12 +478,25 @@
         for d in range(1, nz)
     ]
     got2[z, 0:width, :] = xs[z]
-    for c in ca:
-        c.wait_recv()
-    cb = [send(sv, sall.at[y], sb.at[d], rb.at[d], at_y(d)) for d in range(1, ny)]
-    sall[y] = sv[...]
     for k in range(1, far + 1):
         weight_step(k)
+
+    for c in cb:
+        c.wait_recv()
+    seeds = ny * nz * 8
+    side = sall[...].reshape(seeds, side_ref.shape[1])
+    dl = side[:, :CLASSES]
+    second = side[:, CLASSES:].astype(jnp.int32)
+    taken = lax.broadcasted_iota(jnp.int32, second.shape, 1) < FAN2
+    deg2 = jnp.sum(jnp.where((second >= 0) & taken, 1.0, 0.0), axis=1, keepdims=True)
+    spot = z * LANES + lax.broadcasted_iota(jnp.int32, (seeds, LANES), 1)
+    hits = jnp.zeros((seeds, LANES), F32)
+    for k in range(FAN2):
+        hits = hits + jnp.where(second[:, k : k + 1] == spot, 1.0, 0.0)
+    hits = hits.astype(BF16)
+    at = lax.broadcasted_iota(jnp.int32, (seeds, LANES), 0)
+    row = ((at // 8) % nz) * (ny * 8) + (at // (8 * nz)) * 8 + at % 8
+    same = jnp.where(row == spot, 1.0, 0.0).astype(BF16)
 
     for c in c0 + c2:
         c.wait_recv()
@@ -497,23 +515,6 @@
     c3 = [
         send(pre.at[(y + d) % ny], got3.at[d], s3.at[d], r3.at[d], at_y(d)) for d in range(1, ny)
     ]
-
-    for c in cb:
-        c.wait_recv()
-    seeds = ny * nz * 8
-    side = sall[...].reshape(seeds, side_ref.shape[1])
-    dl = side[:, :CLASSES]
-    second = side[:, CLASSES:].astype(jnp.int32)
-    taken = lax.broadcasted_iota(jnp.int32, second.shape, 1) < FAN2
-    deg2 = jnp.sum(jnp.where((second >= 0) & taken, 1.0, 0.0), axis=1, keepdims=True)
-    spot = z * LANES + lax.broadcasted_iota(jnp.int32, (seeds, LANES), 1)
-    hits = jnp.zeros((seeds, LANES), F32)
-    for k in range(FAN2):
-        hits = hits + jnp.where(second[:, k : k + 1] == spot, 1.0, 0.0)
-    hits = hits.astype(BF16)
-    at = lax.broadcasted_iota(jnp.int32, (seeds, LANES), 0)
-    row = ((at // 8) % nz) * (ny * 8) + (at // (8 * nz)) * 8 + at % 8
-    same = jnp.where(row == spot, 1.0, 0.0).astype(BF16)
 
     def exact(wide, ones):
         total = jnp.zeros((wide.shape[1], ones.shape[1]), F32)
@@ -675,6 +676,26 @@
     )(feats, front, rest, pairs, deg, w, side, b1, w2s, w2n, b2)
 
 
+def finish_kernel(all_ref, logits_ref, gs_ref, gn_ref):
+    cdim = gs_ref.shape[0]
+    gs_ref[...] = all_ref[0:cdim, :]
+    gn_ref[...] = all_ref[CLASSES : CLASSES + cdim, :]
+    logits_ref[0] = all_ref[2 * CLASSES : 2 * CLASSES + 8, 0:cdim]
+
+
+def finish(out, cdim):
+    vmem = pl.BlockSpec(memory_space=pltpu.VMEM)
+    grads = jax.ShapeDtypeStruct((cdim, out.shape[1]), F32)
+    return pl.pallas_call(
+        finish_kernel,
+        out_shape=(jax.ShapeDtypeStruct((1, 8, cdim), F32), grads, grads),
+        in_specs=[vmem],
+        out_specs=(vmem, vmem, vmem),
+        compiler_params=pltpu.CompilerParams(vmem_limit_bytes=VMEM_BYTES),
+        name="finish",
+    )(out)
+
+
 def on_device(feats, front_ids, nbr1, nbr2, w1_self, w1_neigh, b1, w2_self, w2_neigh, b2, dlogits):
     nb, targets, fan = nbr1.shape
     width, verts = feats.shape
@@ -691,11 +712,8 @@
         nz, ny, feats, front, rest, pairs, deg, w, side,
         b1.reshape(ny, 1, LANES), w2_self.T, w2_neigh.T, b2.reshape(1, cdim),
     )
-    return (
-        out[None, 2 * CLASSES :, :cdim],
-        out[:cdim].T,
-        out[CLASSES : CLASSES + cdim].T,
-    )
+    logits, grad_s, grad_n = finish(out, cdim)
+    return (logits, grad_s.T, grad_n.T)
 
 
 def solution(mesh):

time: 84.6 us -> 83.6 us (0.988)
  local copies, waits for them, and re-layouts: 3.24 us -> 0 us
  Pallas kernels: 80.5 us -> 82.4 us
    pallas_call x0 -> x1, Pallas kernels: none -> 1.95 us  [finish(): pl.pallas_call(finish_kernel, out_shape=(jax.ShapeDtypeStruct((1, 8, cdim...]
    transpose x1 -> x0, local copies, waits for them, and re-layouts: 1.95 us -> none  [on_device(): out[CLASSES:CLASSES + cdim]]
    broadcast_in_dim x1 -> x0, local copies, waits for them, and re-layouts: 1.3 us -> none  [on_device(): out[None, 2 * CLASSES:, :cdim]]
    pallas_call x1, Pallas kernels: 19.1 us -> 18 us  [gather(): pl.pallas_call(functools.partial(gather_kernel, nb), out_shape=(jax.Shape...]
    pallas_call x1, Pallas kernels: 61.4 us -> 62.4 us  [layers(): pl.pallas_call(functools.partial(layers_kernel, nz, ny), out_shape=jax.Sh...]
where the time goes in v6:
time: 83.6 us; the launch traced here: 83 us
  Pallas kernels  82.4 us (99%)
    pallas_call x1, Pallas kernels, layers(): pl.pallas_call(functools.partial(layers_kernel, nz, ny), out_shape=jax.Sh...  62.4 us
    pallas_call x1, Pallas kernels, gather(): pl.pallas_call(functools.partial(gather_kernel, nb), out_shape=(jax.Shape...  18 us
    pallas_call x1, Pallas kernels, finish(): pl.pallas_call(finish_kernel, out_shape=(jax.ShapeDtypeStruct((1, 8, cdim...  1.95 us

profile of v6, /device:TPU:1, one launch (start us, length us, event | category | flops | bytes accessed | tf_op | source)
XLA Modules:
  0.0 83.0 jit_solution(12226056671148761639)
XLA Ops:
  0.6 18.0 %neighbour_sums.1 = (f32[8,192,128]{2,1,0:T(8,128)}, s32[64,128]{1,0:T(8,128)}, f32[1,1024]{1,0:T(1,128)}, bf16[48,512]{1,0:T(8,128)(2,1)}, f32[8,176]{1,0:T(8,128)}) custom-call(bf16[24,16384]{1,0:T(8,128)(2,1)} %feats_hbm.3, s32[32768]{0:T(1024)} %bitcast.10, s32[8,1,4096]{2,1,0:T(1,128)} %ids_hbm.1, s32[25,8,1024]{2,1,0:T(8,128)} %bitcast.12, ...), custom_call_target="tpu_custom_call" | custom-call | flops 200000000 | bytes 100000000 | tf_op jit(solution)/shard_map/neighbour_sums/pallas_call | solution.py:262
  18.6 62.4 %layers.1.all_ref = f32[328,512]{1,0:T(8,128)} custom-call(bf16[24,16384]{1,0:T(8,128)(2,1)} %feats_hbm.3, s32[32768]{0:T(1024)} %bitcast.11, f32[8,192,128]{2,1,0:T(8,128)} %get-tuple-element.11.rest_hbm, s32[64,128]{1,0:T(8,128)} %get-tuple-element.12.pairs_hbm, f32[1,1024]{1,0:T(1,128)} %get-tuple-element.13.deg_hbm, ...), custom_call_target="tpu_custom_call" | custom-call | flops 300000000 | bytes 10000000 | tf_op jit(solution)/shard_map/layers/pallas_call | solution.py:627
  81.1 1.9 %finish.1 = (f32[1,8,153]{2,1,0:T(8,128)}, f32[153,512]{1,0:T(8,128)}, f32[153,512]{1,0:T(8,128)}) custom-call(f32[328,512]{1,0:T(8,128)} %layers.1.all_ref), custom_call_target="tpu_custom_call" | custom-call | tf_op jit(solution)/shard_map/finish/pallas_call | solution.py:689
